TPU v7x, 256 devices: a whole 4x4x8 slice. The times are simulated.
256 devices in a mesh: illum: 32 (over x, z), slab: 8 (over y, core).
Axes of the slice: x: 4, y: 4, z: 8, core: 2. Of those that a mesh axis runs over, the one named last changes fastest.
Arguments:
- angles: int32 [32, 2], P('illum'), may hold values from -16 to 16
- contrast: float32 [8, 256, 256], P('slab', 'illum'), may hold values from 0.003 to 0.15
- measured: float32 [32, 2, 256, 256], P('illum'), may hold values from -3.2 to 3.2
Outputs:
- fields: float32 [32, 2, 8, 256, 256], P('illum', None, 'slab')
- descent: float32 [8, 256, 256], P('slab', 'illum')
- misfit: float32 [], replicated
All inputs are finite; a program needn't handle non-finite values.
Results may differ from a plain program's by a relative error of at most 0.0003.
Values sent between devices are 32-bit elements; how exact they have to be, the bound alone decides.
A program may use at most 64 MiB of HBM per device.

v0:
```python
import math

import jax
import jax.numpy as jnp
from jax import lax
from jax.sharding import PartitionSpec as P

ITERS = 2


wave_number = 2.0 * math.pi / 8.0
damping = 0.2
tilt_step = 0.04
highest_precision = lax.Precision.HIGHEST


def symbol(indices, length):
    return 2.0 - 2.0 * jnp.cos(2.0 * math.pi / length * indices.astype(jnp.float32))


def depth_kernel(distance, transverse):
    squared = wave_number * wave_number
    shifted = transverse - squared
    loss_term = squared * damping
    radius = jnp.sqrt(shifted * shifted + loss_term * loss_term)
    decay_rate = jnp.sqrt(0.5 * (radius + shifted))
    turn_rate = jnp.sqrt(0.5 * (radius - shifted))
    scale = squared / (2.0 * radius) * jnp.exp(-decay_rate * distance)
    cosine_part = jnp.cos(turn_rate * distance)
    sine_part = jnp.sin(turn_rate * distance)
    return (
        scale * (decay_rate * cosine_part - turn_rate * sine_part),
        -scale * (decay_rate * sine_part + turn_rate * cosine_part),
    )


def matrix_pair(length, orientation):
    indices = jnp.arange(length, dtype=jnp.int32)
    radians = (
        2.0 * math.pi / length * (indices[:, None] * indices[None, :] % length).astype(jnp.float32)
    )
    return (jnp.cos(radians), orientation * jnp.sin(radians))


def fourier_transform(values, pair_table, einsum_form):
    cosine_table, sine_table = pair_table
    cosine_term = jnp.einsum(einsum_form, values, cosine_table, precision=highest_precision)
    sine_term = jnp.einsum(einsum_form, values, sine_table, precision=highest_precision)
    return jnp.stack([cosine_term[0] - sine_term[1], sine_term[0] + cosine_term[1]])


def body(angles, contrast, measured):
    contrast = lax.all_gather(contrast, "illum", axis=1, tiled=True)
    depth_local, breadth, extent = contrast.shape
    slab_count = lax.axis_size("slab")
    depth = depth_local * slab_count
    slab_index = lax.axis_index("slab")
    part_rows = breadth // slab_count
    forward_y = matrix_pair(extent, -1.0)
    inverse_transform_y = matrix_pair(extent, 1.0)
    forward_x = matrix_pair(breadth, -1.0)
    inverse_transform_x = matrix_pair(breadth, 1.0)
    wave_z = jnp.arange(depth, dtype=jnp.int32)
    wave_x = slab_index * part_rows + jnp.arange(part_rows, dtype=jnp.int32)
    wave_y = jnp.arange(extent, dtype=jnp.int32)
    row_transverse = symbol(wave_x, breadth)[:, None] + symbol(wave_y, extent)[None, :]
    distances = jnp.abs(wave_z[:, None] - wave_z[None, :]).astype(jnp.float32)
    coupling_real, coupling_imaginary = depth_kernel(
        distances[:, :, None, None], row_transverse[None, None]
    )
    inverse_norm = 1.0 / (breadth * extent)

    def depth_sum(column_list, orientation):
        real_part = column_list[0]
        imaginary_part = column_list[1]
        real_real = jnp.einsum(
            "zwxy,wxy->zxy", coupling_real, real_part, precision=highest_precision
        )
        imag_imag = jnp.einsum(
            "zwxy,wxy->zxy", coupling_imaginary, imaginary_part, precision=highest_precision
        )
        real_imag = jnp.einsum(
            "zwxy,wxy->zxy", coupling_real, imaginary_part, precision=highest_precision
        )
        imag_real = jnp.einsum(
            "zwxy,wxy->zxy", coupling_imaginary, real_part, precision=highest_precision
        )
        return jnp.stack([real_real - orientation * imag_imag, real_imag + orientation * imag_real])

    def convolve(values, orientation):
        spectral = fourier_transform(
            fourier_transform(values, forward_y, "lsmu,ue->lsme"), forward_x, "adhb,he->adeb"
        )
        column_list = lax.all_to_all(spectral, "slab", split_axis=2, concat_axis=1, tiled=True)
        column_list = depth_sum(column_list, orientation)
        slab_layout = lax.all_to_all(column_list, "slab", split_axis=1, concat_axis=2, tiled=True)
        spatial = fourier_transform(
            fourier_transform(slab_layout, inverse_transform_x, "adhb,he->adeb"),
            inverse_transform_y,
            "lsmu,ue->lsme",
        )
        return spatial * inverse_norm

    def adjoint(values):
        return values - contrast * convolve(values, -1.0)

    tilts = jnp.sin(tilt_step * angles[0].astype(jnp.float32))
    sine_x = tilts[0]
    sine_y = tilts[1]
    cosine_z = jnp.sqrt(1.0 - sine_x * sine_x - sine_y * sine_y)
    z_global = slab_index * depth_local + jnp.arange(depth_local, dtype=jnp.int32)
    z_position = z_global.astype(jnp.float32)
    x_coordinate = jnp.arange(breadth, dtype=jnp.int32).astype(jnp.float32)
    y_position = wave_y.astype(jnp.float32)
    phases = wave_number * (
        sine_x * x_coordinate[None, :, None]
        + sine_y * y_position[None, None, :]
        + cosine_z * z_position[:, None, None]
    )
    incident = jnp.stack([jnp.cos(phases), jnp.sin(phases)])
    solution = incident
    residual = convolve(contrast * incident, 1.0)
    gradient_dir = adjoint(residual)
    direction = gradient_dir
    norm_now = lax.psum(jnp.sum(gradient_dir * gradient_dir), "slab")
    for iteration in range(ITERS):
        mapped = direction - convolve(contrast * direction, 1.0)
        step_size = norm_now / lax.psum(jnp.sum(mapped * mapped), "slab")
        solution = solution + step_size * direction
        if iteration + 1 < ITERS:
            residual = residual - step_size * mapped
            gradient_dir = adjoint(residual)
            norm_next = lax.psum(jnp.sum(gradient_dir * gradient_dir), "slab")
            direction = gradient_dir + norm_next / norm_now * direction
            norm_now = norm_next
    is_last = slab_index == slab_count - 1
    mismatch = solution[:, depth_local - 1] - incident[:, depth_local - 1] - measured[0]
    misfit_local = jnp.where(is_last, 0.5 * jnp.sum(mismatch * mismatch), 0.0)
    detector = jnp.where(is_last, mismatch, 0.0)
    source_field = jnp.concatenate(
        [jnp.zeros((2, depth_local - 1, breadth, extent), jnp.float32), detector[:, None]], axis=1
    )
    back_field = convolve(source_field, -1.0)
    partial_value = solution[0] * back_field[0] + solution[1] * back_field[1]
    gradient_rows = lax.psum_scatter(partial_value, "illum", scatter_dimension=1, tiled=True)
    square_sum, misfit = lax.psum(
        (jnp.sum(gradient_rows * gradient_rows), misfit_local), ("illum", "slab")
    )
    mean_square = square_sum / (depth * breadth * extent)
    descent = gradient_rows / jnp.sqrt(mean_square + 1e-06)
    return (solution[None], descent, misfit)


def solution(mesh):
    return jax.shard_map(
        body,
        mesh=mesh,
        in_specs=(P("illum", None), P("slab", "illum", None), P("illum", None, None, None)),
        out_specs=(P("illum", None, "slab", None, None), P("slab", "illum", None), P()),
        check_vma=False,
    )
```

profile of v0, /device:TPU:1, one launch (start us, length us, event | category | flops | bytes accessed | tf_op | source)
XLA Modules:
  0.0 719.7 jit_solution(3585343545429761142)
XLA Ops:
  12.4 40.8 %all_gather.3 = f32[1,256,256]{2,1,0:T(8,128)S(1)} all-gather(f32[1,8,256]{2,1,0:T(8,128)} %param.4), channel_id=1, replica_groups=mesh['illum'=32,'slab'=8] {'illum'}, dimensions={1}, use_global_device_ids=true | all-gather | bytes 270336 | tf_op jit(solution)/shard_map/all_gather | solution.py:53
  53.3 2.0 fusion.151
  63.0 17.5 %all-to-all-start = ((f32[2,1,256,256]{3,0,1,2:T(2,128)}), f32[2,1,256,256]{3,0,1,2:T(2,128)S(1)}, u32[]{:S(2)}, u32[]{:S(2)}) async-start(f32[2,1,256,256]{3,0,1,2:T(2,128)} %copy.32), calls=%async_computation | async-start | bytes 1048576 | tf_op jit(solution)/shard_map/all_to_all | solution.py:94
  80.7 9.2 %all-to-all-done = f32[2,1,256,256]{3,0,1,2:T(2,128)S(1)} async-done(((f32[2,1,256,256]{3,0,1,2:T(2,128)}), f32[2,1,256,256]{3,0,1,2:T(2,128)S(1)}, u32[]{:S(2)}, u32[]{:S(2)}) %all-to-all-start) | async-done | bytes 524320 | tf_op jit(solution)/shard_map/all_to_all | solution.py:94
  90.4 9.3 %multiply_reduce_fusion.22 = (f32[32,256,8]{1,0,2:T(8,128)S(1)}, f32[32,256,8]{1,0,2:T(8,128)S(1)}, f32[32,256,8]{1,0,2:T(8,128)S(1)}, f32[32,256,8]{1,0,2:T(8,128)S(1)}) fusion(f32[32,256,8]{1,0,2:T(8,128)S(1)} %bitcast.576, f32[32,256]{1,0:T(8,128)S(1)} %get-tuple-element.120, f32[32,256]{1,0:T(8,128)S(1)} %get-tuple-element.121, ...), kind=kLoop, calls=%fused_computation.34 | loop fusion | flops 10223616 | bytes 1704192 | tf_op jit(solution)/shard_map/zwxy,wxy->zxy/dot_general | solution.py:79
  99.9 12.6 %all_to_all.48 = f32[2,8,32,256]{3,2,0,1:T(8,128)S(1)} all-to-all(f32[2,8,32,256]{3,2,0,1:T(8,128)S(1)} %pad_maximum_fusion.2), channel_id=1, replica_groups=mesh['illum'=32,'slab'=8] {'slab'}, dimensions={1} | all-to-all | bytes 1048576 | tf_op jit(solution)/shard_map/all_to_all | solution.py:96
  123.7 2.0 convolution_bitcast_fusion.18
  126.3 12.8 %all_to_all.49 = f32[2,1,256,256]{3,0,1,2:T(2,128)S(1)} all-to-all(f32[2,1,256,256]{3,0,1,2:T(2,128)S(1)} %copy.38), channel_id=1, replica_groups=mesh['illum'=32,'slab'=8] {'slab'}, dimensions={2} | all-to-all | bytes 1048576 | tf_op jit(solution)/shard_map/all_to_all | solution.py:94
  139.5 9.3 %multiply_reduce_fusion.18 = (f32[32,256,8]{1,0,2:T(8,128)S(1)}, f32[32,256,8]{1,0,2:T(8,128)S(1)}, f32[32,256,8]{1,0,2:T(8,128)S(1)}, f32[32,256,8]{1,0,2:T(8,128)S(1)}) fusion(f32[32,256,8]{1,0,2:T(8,128)S(1)} %bitcast.572, f32[32,256]{1,0:T(8,128)S(1)} %get-tuple-element.120, f32[32,256]{1,0:T(8,128)S(1)} %get-tuple-element.121, ...), kind=kLoop, calls=%fused_computation.30 | loop fusion | flops 10223616 | bytes 1704192 | tf_op jit(solution)/shard_map/zwxy,wxy->zxy/dot_general | solution.py:79
  149.8 4.4 all-to-all-start.3
  154.2 9.5 %all-to-all-done.3 = f32[2,8,32,256]{3,2,0,1:T(8,128)S(1)} async-done(((f32[2,8,32,256]{3,2,0,1:T(8,128)}), f32[2,8,32,256]{3,2,0,1:T(8,128)S(1)}, u32[]{:S(2)}, u32[]{:S(2)}) %all-to-all-start.3) | async-done | bytes 524320 | tf_op jit(solution)/shard_map/all_to_all | solution.py:96
  177.3 12.6 %all_to_all.50 = f32[2,1,256,256]{3,0,1,2:T(2,128)S(1)} all-to-all(f32[2,1,256,256]{3,0,1,2:T(2,128)S(1)} %copy.45), channel_id=1, replica_groups=mesh['illum'=32,'slab'=8] {'slab'}, dimensions={2} | all-to-all | bytes 1048576 | tf_op jit(solution)/shard_map/all_to_all | solution.py:94
  190.4 9.3 %multiply_reduce_fusion.14 = (f32[32,256,8]{1,0,2:T(8,128)S(1)}, f32[32,256,8]{1,0,2:T(8,128)S(1)}, f32[32,256,8]{1,0,2:T(8,128)S(1)}, f32[32,256,8]{1,0,2:T(8,128)S(1)}) fusion(f32[32,256,8]{1,0,2:T(8,128)S(1)} %bitcast.578, f32[32,256]{1,0:T(8,128)S(1)} %get-tuple-element.120, f32[32,256]{1,0:T(8,128)S(1)} %get-tuple-element.121, ...), kind=kLoop, calls=%fused_computation.26 | loop fusion | flops 10223616 | bytes 1704192 | tf_op jit(solution)/shard_map/zwxy,wxy->zxy/dot_general | solution.py:79
  199.9 12.8 %all_to_all.51 = f32[2,8,32,256]{3,2,0,1:T(8,128)S(1)} all-to-all(f32[2,8,32,256]{3,2,0,1:T(8,128)S(1)} %pad_maximum_fusion.6), channel_id=1, replica_groups=mesh['illum'=32,'slab'=8] {'slab'}, dimensions={1} | all-to-all | bytes 1048576 | tf_op jit(solution)/shard_map/all_to_all | solution.py:96
  220.0 13.6 %all-reduce.1 = (f32[]{:T(128)}, f32[]{:T(128)}) all-reduce(f32[]{:T(128)} %get-tuple-element.4, f32[]{:T(128)} %get-tuple-element.3), channel_id=1, replica_groups=mesh['illum'=32,'slab'=8] {'slab'}, use_global_device_ids=true, to_apply=%region_1.2 | all-reduce | flops 2 | bytes 16 | tf_op jit(solution)/shard_map/psum | solution.py:125
  242.0 12.6 %all_to_all.52 = f32[2,1,256,256]{3,0,1,2:T(2,128)S(1)} all-to-all(f32[2,1,256,256]{3,0,1,2:T(2,128)S(1)} %copy.51), channel_id=1, replica_groups=mesh['illum'=32,'slab'=8] {'slab'}, dimensions={2} | all-to-all | bytes 1048576 | tf_op jit(solution)/shard_map/all_to_all | solution.py:94
  255.1 9.3 %multiply_reduce_fusion.10 = (f32[32,256,8]{1,0,2:T(8,128)S(1)}, f32[32,256,8]{1,0,2:T(8,128)S(1)}, f32[32,256,8]{1,0,2:T(8,128)S(1)}, f32[32,256,8]{1,0,2:T(8,128)S(1)}) fusion(f32[32,256,8]{1,0,2:T(8,128)S(1)} %bitcast.579, f32[32,256]{1,0:T(8,128)S(1)} %get-tuple-element.120, f32[32,256]{1,0:T(8,128)S(1)} %get-tuple-element.121, ...), kind=kLoop, calls=%fused_computation.22 | loop fusion | flops 10223616 | bytes 1704192 | tf_op jit(solution)/shard_map/zwxy,wxy->zxy/dot_general | solution.py:79
  264.6 13.2 %all_to_all.53 = f32[2,8,32,256]{3,2,0,1:T(8,128)S(1)} all-to-all(f32[2,8,32,256]{3,2,0,1:T(8,128)S(1)} %copy.52), channel_id=1, replica_groups=mesh['illum'=32,'slab'=8] {'slab'}, dimensions={1} | all-to-all | bytes 1048576 | tf_op jit(solution)/shard_map/all_to_all | solution.py:96
  285.1 13.6 %psum.44 = f32[]{:T(128)} all-reduce(f32[]{:T(128)} %get-tuple-element.47), channel_id=1, replica_groups=mesh['illum'=32,'slab'=8] {'slab'}, use_global_device_ids=true, to_apply=%region_5.6 | all-reduce | flops 1 | bytes 8 | tf_op jit(solution)/shard_map/psum | solution.py:133
  308.3 12.6 %all_to_all.54 = f32[2,1,256,256]{3,0,1,2:T(2,128)S(1)} all-to-all(f32[2,1,256,256]{3,0,1,2:T(2,128)S(1)} %copy.58), channel_id=1, replica_groups=mesh['illum'=32,'slab'=8] {'slab'}, dimensions={2} | all-to-all | bytes 1048576 | tf_op jit(solution)/shard_map/all_to_all | solution.py:94
  321.4 9.3 %multiply_reduce_fusion.6 = (f32[32,256,8]{1,0,2:T(8,128)S(1)}, f32[32,256,8]{1,0,2:T(8,128)S(1)}, f32[32,256,8]{1,0,2:T(8,128)S(1)}, f32[32,256,8]{1,0,2:T(8,128)S(1)}) fusion(f32[32,256,8]{1,0,2:T(8,128)S(1)} %bitcast.580, f32[32,256]{1,0:T(8,128)S(1)} %get-tuple-element.120, f32[32,256]{1,0:T(8,128)S(1)} %get-tuple-element.121, ...), kind=kLoop, calls=%fused_computation.18 | loop fusion | flops 10223616 | bytes 1704192 | tf_op jit(solution)/shard_map/zwxy,wxy->zxy/dot_general | solution.py:79
  331.6 5.3 all-to-all-start.9
  338.8 7.7 %all-to-all-done.9 = f32[2,8,32,256]{3,2,0,1:T(8,128)} async-done(((f32[2,8,32,256]{3,2,0,1:T(8,128)}), f32[2,8,32,256]{3,2,0,1:T(8,128)}, u32[]{:S(2)}, u32[]{:S(2)}) %all-to-all-start.9) | async-done | bytes 524320 | tf_op jit(solution)/shard_map/all_to_all | solution.py:96
  354.7 13.6 %psum.45 = f32[]{:T(128)} all-reduce(f32[]{:T(128)} %fusion.23), channel_id=1, replica_groups=mesh['illum'=32,'slab'=8] {'slab'}, use_global_device_ids=true, to_apply=%region_7.8 | all-reduce | flops 1 | bytes 8 | tf_op jit(solution)/shard_map/psum | solution.py:128
  369.7 2.1 multiply_reduce_fusion.24
  378.8 12.8 %all_to_all.55 = f32[2,1,256,256]{3,0,1,2:T(2,128)S(1)} all-to-all(f32[2,1,256,256]{3,0,1,2:T(2,128)S(1)} %copy.64), channel_id=1, replica_groups=mesh['illum'=32,'slab'=8] {'slab'}, dimensions={2} | all-to-all | bytes 1048576 | tf_op jit(solution)/shard_map/all_to_all | solution.py:94
  392.0 9.3 %multiply_reduce_fusion.2 = (f32[32,256,8]{1,0,2:T(8,128)S(1)}, f32[32,256,8]{1,0,2:T(8,128)S(1)}, f32[32,256,8]{1,0,2:T(8,128)S(1)}, f32[32,256,8]{1,0,2:T(8,128)S(1)}) fusion(f32[32,256,8]{1,0,2:T(8,128)S(1)} %bitcast.570, f32[32,256]{1,0:T(8,128)S(1)} %get-tuple-element.120, f32[32,256]{1,0:T(8,128)S(1)} %get-tuple-element.121, ...), kind=kLoop, calls=%fused_computation.14 | loop fusion | flops 10223616 | bytes 1704192 | tf_op jit(solution)/shard_map/zwxy,wxy->zxy/dot_general | solution.py:79
  402.3 4.4 all-to-all-start.11
  406.9 1.9 fusion.30
  408.9 7.4 %all-to-all-done.11 = f32[2,8,32,256]{3,2,0,1:T(8,128)S(1)} async-done(((f32[2,8,32,256]{3,2,0,1:T(8,128)}), f32[2,8,32,256]{3,2,0,1:T(8,128)S(1)}, u32[]{:S(2)}, u32[]{:S(2)}) %all-to-all-start.11) | async-done | bytes 524320 | tf_op jit(solution)/shard_map/all_to_all | solution.py:96
  425.2 203.9 %reduce-scatter.2.cloned.1.call-done = f32[1,8,256]{2,1,0:T(8,128)} async-done(((f32[1,256,256]{2,1,0:T(8,128)}), f32[1,8,256]{2,1,0:T(8,128)}) %reduce-scatter.2.cloned.1.call-update) | async-done | bytes 8208 | tf_op jit(solution)/shard_map/reduce_scatter | solution.py:145
  631.5 79.9 %all-reduce = (f32[]{:T(128)}, f32[]{:T(128)}) all-reduce(f32[]{:T(128)} %multiply_reduce_fusion.28, f32[]{:T(128)S(6)} %select_n.124), channel_id=1, replica_groups=mesh['illum'=32,'slab'=8] {'illum','slab'}, use_global_device_ids=true, to_apply=%region_10.11 | all-reduce | flops 2 | bytes 16 | tf_op jit(solution)/shard_map/psum | solution.py:146
  (172 shorter events, 99.4 us)
Async XLA Ops:
  53.2 118.5 %copy-start.4 = (f32[1,256,256]{2,1,0:T(8,128)}, f32[1,256,256]{2,1,0:T(8,128)S(1)}, u32[]{:S(2)}) copy-start(f32[1,256,256]{2,1,0:T(8,128)S(1)} %all_gather.3) | copy-start | bytes 786436
  55.2 1.6 copy-start.7
  55.3 1.6 copy-start.8
  63.0 27.0 %all-to-all-start = ((f32[2,1,256,256]{3,0,1,2:T(2,128)}), f32[2,1,256,256]{3,0,1,2:T(2,128)S(1)}, u32[]{:S(2)}, u32[]{:S(2)}) async-start(f32[2,1,256,256]{3,0,1,2:T(2,128)} %copy.32), calls=%async_computation | async-start | bytes 1048576 | tf_op jit(solution)/shard_map/all_to_all | solution.py:94
  149.8 13.9 %all-to-all-start.3 = ((f32[2,8,32,256]{3,2,0,1:T(8,128)}), f32[2,8,32,256]{3,2,0,1:T(8,128)S(1)}, u32[]{:S(2)}, u32[]{:S(2)}) async-start(f32[2,8,32,256]{3,2,0,1:T(8,128)} %pad_maximum_fusion.4), calls=%async_computation.3 | async-start | bytes 1048576 | tf_op jit(solution)/shard_map/all_to_all | solution.py:96
  284.3 0.8 copy-start
  284.3 0.8 copy-start.2
  300.1 1.3 copy-start.5
  331.6 14.9 %all-to-all-start.9 = ((f32[2,8,32,256]{3,2,0,1:T(8,128)}), f32[2,8,32,256]{3,2,0,1:T(8,128)}, u32[]{:S(2)}, u32[]{:S(2)}) async-start(f32[2,8,32,256]{3,2,0,1:T(8,128)} %pad_maximum_fusion.10), calls=%async_computation.9 | async-start | bytes 1048576 | tf_op jit(solution)/shard_map/all_to_all | solution.py:96
  402.3 13.9 %all-to-all-start.11 = ((f32[2,8,32,256]{3,2,0,1:T(8,128)}), f32[2,8,32,256]{3,2,0,1:T(8,128)S(1)}, u32[]{:S(2)}, u32[]{:S(2)}) async-start(f32[2,8,32,256]{3,2,0,1:T(8,128)} %copy.65), calls=%async_computation.11 | async-start | bytes 1048576 | tf_op jit(solution)/shard_map/all_to_all | solution.py:96
  406.8 222.3 %reduce-scatter.2.cloned.1.call-start = ((), (), s32[]{:S(2)}) async-start(), calls=%async_computation.13 | async-start | bytes 270336 | tf_op jit(solution)/shard_map/reduce_scatter | solution.py:145
  422.7 1.0 copy-start.6
  423.8 206.6 %copy-start.1 = (f32[1,256,256]{2,1,0:T(8,128)S(1)}, f32[1,256,256]{2,1,0:T(8,128)}, u32[]{:S(2)}) copy-start(f32[1,256,256]{2,1,0:T(8,128)} %copy-done) | copy-start | bytes 786436
  423.8 206.6 %copy-start.3 = (f32[1,256,256]{2,1,0:T(8,128)S(1)}, f32[1,256,256]{2,1,0:T(8,128)}, u32[]{:S(2)}) copy-start(f32[1,256,256]{2,1,0:T(8,128)} %copy-done.2) | copy-start | bytes 786436
  423.8 206.6 %copy-start.9 = (f32[1,1,1,256,256]{4,3,2,1,0:T(8,128)S(1)}, f32[1,1,1,256,256]{4,3,2,1,0:T(8,128)}, u32[]{:S(2)}) copy-start(f32[1,1,1,256,256]{4,3,2,1,0:T(8,128)} %get-tuple-element.112) | copy-start | bytes 786436
  423.8 206.6 %copy-start.10 = (f32[1,1,1,256,256]{4,3,2,1,0:T(8,128)S(1)}, f32[1,1,1,256,256]{4,3,2,1,0:T(8,128)}, u32[]{:S(2)}) copy-start(f32[1,1,1,256,256]{4,3,2,1,0:T(8,128)} %get-tuple-element.114) | copy-start | bytes 786436
  630.4 81.7 %copy-start.11 = (f32[1,8,256]{2,1,0:T(8,128)S(1)}, f32[1,8,256]{2,1,0:T(8,128)}, u32[]{:S(2)}) copy-start(f32[1,8,256]{2,1,0:T(8,128)} %reduce-scatter.2.cloned.1.call-done) | copy-start | bytes 24580
Sparse Core Ops, SparseCore 0:
  424.7 204.3 reduce-scatter.1
where the time goes:
time: 727 us; the launch traced here: 720 us
  blocking collectives  264 us (36%)
  waiting for transfers between devices  238 us (33%)
  other arithmetic  77.6 us (11%)
  matrix products  75.7 us (10%)
  starting transfers between devices  31.9 us (4%)
  between operations  23.3 us (3%)
  local copies, waits for them, and re-layouts  9.69 us (1%)
    reduce_scatter x1, waiting for transfers between devices, body(): lax.psum_scatter(partial_value, 'illum', scatter_dimension=1, tiled=True)  204 us
    psum x1, blocking collectives, body(): lax.psum((jnp.sum(gradient_rows * gradient_rows), misfit_local), ('illum'...  79.9 us
    all_to_all x5, blocking collectives, convolve(): lax.all_to_all(spectral, 'slab', split_axis=2, concat_axis=1, tiled=True)  63.5 us
    dot_general x6, other arithmetic, depth_sum(): jnp.einsum('zwxy,wxy->zxy', coupling_imaginary, imaginary_part, precision...  55.8 us
    all_gather x1, blocking collectives, body(): contrast = lax.all_gather(contrast, 'illum', axis=1, tiled=True)  40.8 us
    all_to_all x3, blocking collectives, convolve(): lax.all_to_all(column_list, 'slab', split_axis=1, concat_axis=2, tiled=True)  38.6 us
    dot_general x24, matrix products, fourier_transform(): jnp.einsum(einsum_form, values, sine_table, precision=highest_precision)  38.4 us
    dot_general x24, matrix products, fourier_transform(): jnp.einsum(einsum_form, values, cosine_table, precision=highest_precision)  37.4 us
  transfers between devices with their start and end apart: 5, of which 5 were waited for; matrix products, arithmetic and copies ran while one was open for 1% of the time, Pallas kernels for 0%

commit v1 on v0

v1 whole, which is shorter than its diff:
```python
import functools
import math

import jax
import jax.numpy as jnp
import ml_dtypes
import numpy as np
from jax import lax
from jax.experimental import pallas as pl
from jax.experimental.pallas import tpu as pltpu
from jax.sharding import PartitionSpec as P

MESH = pl.DeviceIdType.MESH
N = 256
H = 128
NZ = 8
ILLUMS = 32
WAVE = 2.0 * math.pi / 8.0
DAMPING = 0.2
TILT = 0.04
CHUNKS = 4
CR = 64


def split_np(m):
    hi = m.astype(ml_dtypes.bfloat16)
    lo = (m - hi.astype(np.float64)).astype(ml_dtypes.bfloat16)
    return np.stack([hi, lo])


def dft_tables():
    n = np.arange(H)[:, None]
    m = np.arange(H)[None, :]
    out = []
    for q in (0, 1):
        theta = -2.0 * np.pi / N * ((n * (2 * m + q)) % N)
        c, s = np.cos(theta), np.sin(theta)
        out.append(np.block([[c, s], [-s, c]]))
    right = np.stack([split_np(r) for r in out])
    left = np.stack([split_np(np.ascontiguousarray(r.T)) for r in out])
    return right, left


def depth_tables():
    order = np.concatenate([np.arange(0, N, 2), np.arange(1, N, 2)])
    sym = 2.0 - 2.0 * np.cos(2.0 * np.pi / N * order)
    b = WAVE * WAVE
    p = sym[:, None] + sym[None, :] - b
    l = b * DAMPING
    r = np.sqrt(p * p + l * l)
    qr = np.sqrt((r + p) / 2.0)
    qi = l / (2.0 * qr)
    w = np.exp(-(qr + 1j * qi))
    g = b / (2.0 * r) * (qr - 1j * qi)

    def pack(t):
        t = t.reshape(2, H, N)
        return np.stack([t.real, t.imag], axis=1).astype(np.float32)

    source = np.stack([pack(np.conj(g * w ** (NZ - 1 - s))) for s in range(NZ)])
    return np.stack([pack(w), pack(g)]), source


def split(a):
    hi = a.astype(jnp.bfloat16)
    lo = (a - hi.astype(jnp.float32)).astype(jnp.bfloat16)
    return hi, lo


def dot_right(a, m_ref, q):
    hi, lo = split(a)
    mh, ml = m_ref[q, 0], m_ref[q, 1]
    return jnp.dot(
        jnp.concatenate([hi, lo, hi], axis=1),
        jnp.concatenate([mh, mh, ml], axis=0),
        preferred_element_type=jnp.float32,
    )


def dot_left(m_ref, q, a):
    hi, lo = split(a)
    mh, ml = m_ref[q, 0], m_ref[q, 1]
    return jnp.dot(
        jnp.concatenate([mh, mh, ml], axis=1),
        jnp.concatenate([hi, lo, hi], axis=0),
        preferred_element_type=jnp.float32,
    )


def forward_plane(re, im, right, left, store):
    halves = []
    for q in (0, 1):
        if q == 0:
            a = jnp.concatenate([re[:, :H] + re[:, H:], im[:, :H] + im[:, H:]], axis=1)
        else:
            a = jnp.concatenate([re[:, :H] - re[:, H:], im[:, :H] - im[:, H:]], axis=1)
        halves.append(dot_right(a, right, q))
    for q in (0, 1):
        parts = []
        for t in halves:
            u = t[:H] + t[H:] if q == 0 else t[:H] - t[H:]
            parts.append(jnp.concatenate([u[:, :H], u[:, H:]], axis=0))
        store(q, dot_left(left, q, jnp.concatenate(parts, axis=1)))


def inverse_plane(load, right, left):
    e = [dot_left(right, q, load(q)) for q in (0, 1)]
    e = [part * (1.0 / (N * N)) for part in e]
    top, bottom = e[0] + e[1], e[0] - e[1]
    re = jnp.concatenate([top[:H], bottom[:H]], axis=0)
    im = jnp.concatenate([top[H:], bottom[H:]], axis=0)
    e = []
    for q in (0, 1):
        z = jnp.concatenate([re[:, q * H : (q + 1) * H], im[:, q * H : (q + 1) * H]], axis=1)
        e.append(dot_right(z, left, q))
    low, high = e[0] + e[1], e[0] - e[1]
    re = jnp.concatenate([low[:, :H], high[:, :H]], axis=1)
    im = jnp.concatenate([low[:, H:], high[:, H:]], axis=1)
    return re, im


def cmul(a, b):
    return a[0] * b[0] - a[1] * b[1], a[0] * b[1] + a[1] * b[0]


def cadd(a, b):
    return a[0] + b[0], a[1] + b[1]


def csub(a, b):
    return a[0] - b[0], a[1] - b[1]


def tile_sum(a):
    a = a[:, :H] + a[:, H:]
    if a.shape[0] > 8:
        a = jnp.sum(a.reshape(a.shape[0] // 8, 8, H), axis=0)
    return a


def total_of(tile):
    return jnp.sum(jnp.sum(tile, axis=0, keepdims=True), axis=1, keepdims=True)


def kernel(
    angles, block, meas, right, left, wg, source_table,
    fields, descent, misfit,
    plane, c4, s_buf, f_buf, w_buf, gh0, gh1, g0, g1, r_buf, ybuf, red_out, red_in,
    mh, h7, part, rs_in, ar_out, ar1, ar2,
    ga_s, ga_r, gb_s, gb_r, x_s, x_r, rd_s, rd_r, pg_s, pg_r, ht_s, ht_r, h7_sem,
    rs_s, rs_r, a1_s, a1_r, a2_s, a2_r,
):
    illum = lax.axis_index("illum")
    slab = lax.axis_index("slab")
    chip = slab // 2
    core = slab - 2 * chip
    other = (illum, slab + 1 - 2 * core)

    def illum_peer(k):
        return (lax.rem(illum + k, ILLUMS), slab)

    def slab_peer(k):
        return (illum, lax.rem(slab + k, NZ))

    load_h7 = pltpu.make_async_copy(source_table.at[slab], h7, h7_sem)
    load_h7.start()

    barrier = pltpu.get_barrier_semaphore()
    for k in range(1, ILLUMS):
        pl.semaphore_signal(barrier, inc=1, device_id=illum_peer(k), device_id_type=MESH)
    for k in range(1, NZ):
        pl.semaphore_signal(barrier, inc=1, device_id=slab_peer(k), device_id_type=MESH)
    pl.semaphore_wait(barrier, ILLUMS - 1 + NZ - 1)

    my_rows = pl.ds(pl.multiple_of(illum * 8, 8), 8)
    for k in range(1, ILLUMS):
        pltpu.make_async_remote_copy(
            src_ref=block, dst_ref=plane.at[my_rows], send_sem=ga_s, recv_sem=ga_r,
            device_id=illum_peer(k), device_id_type=MESH,
        ).start()
    plane[my_rows, :] = block[...]

    def angle_row(i):
        return jnp.sin(TILT * jnp.full((1, H), angles[0, i], jnp.int32).astype(jnp.float32))

    sine_x, sine_y = angle_row(0), angle_row(1)
    cos_z = jnp.sqrt(1.0 - sine_x * sine_x - sine_y * sine_y)
    x_at = lax.broadcasted_iota(jnp.int32, (N, H), 0).astype(jnp.float32)
    x_phase = WAVE * (sine_x * x_at)
    ex = jnp.cos(x_phase), jnp.sin(x_phase)
    y_at = lax.broadcasted_iota(jnp.int32, (1, H), 1).astype(jnp.float32)

    def incident(z):
        halves = []
        zf = jnp.full((1, H), z, jnp.int32).astype(jnp.float32)
        for q in (0, 1):
            phase = WAVE * (sine_y * (y_at + float(q * H)) + cos_z * zf)
            halves.append(cmul(ex, (jnp.cos(phase), jnp.sin(phase))))
        return tuple(jnp.concatenate([halves[0][i], halves[1][i]], axis=1) for i in (0, 1))

    def store_to(ref, p):
        def store(q, value):
            ref[p, q, 0] = value[:H]
            ref[p, q, 1] = value[H:]
        return store

    def load_from(ref, p):
        return lambda q: jnp.concatenate([ref[p, q, 0], ref[p, q, 1]], axis=0)

    def store_mh(q, value):
        mh[q, 0] = value[:H]
        mh[q, 1] = value[H:]

    forward_plane(meas[0], meas[1], right, left, store_mh)

    def sent(n, src, dst, s_sem, r_sem, dev):
        return pltpu.make_async_remote_copy(
            src_ref=src, dst_ref=dst, send_sem=s_sem, recv_sem=r_sem, device_id=dev, device_id_type=MESH
        )

    def wait_bytes(ref, sem):
        pltpu.make_async_copy(ref, ref, sem).wait()

    wait_bytes(plane.at[pl.ds(0, (ILLUMS - 1) * 8)], ga_s)
    wait_bytes(plane.at[pl.ds(0, (ILLUMS - 1) * 8)], ga_r)

    high = slab // 4
    slot = slab + high * (7 - 2 * slab)
    for k in range(1, 4):
        dest = 2 * lax.rem(chip + k, 4) + high
        sent(0, plane, c4.at[slot], gb_s.at[k], gb_r.at[slot], (illum, dest)).start()

    @pl.when(core != high)
    def _():
        sent(0, plane, c4.at[slot], gb_s.at[0], gb_r.at[slot], other).start()

    @pl.when(core == high)
    def _():
        c4[slot] = plane[...]

    for k in range(1, 4):
        sent(0, plane, c4.at[slot], gb_s.at[k], gb_r.at[slot], other).wait_send()

    @pl.when(core != high)
    def _():
        sent(0, plane, c4.at[slot], gb_s.at[0], gb_r.at[slot], other).wait_send()

    for k in range(4):
        @pl.when((core != high) | (slot != k))
        def _():
            sent(0, plane, c4.at[k], gb_s.at[0], gb_r.at[k], other).wait_recv()

    def global_z(k):
        return k + core * (7 - 2 * k)

    @pl.loop(0, 4)
    def _(p):
        re, im = incident(global_z(p))
        c = c4[p]
        forward_plane(c * re, c * im, right, left, store_to(s_buf, p))

    def where_q(q):
        return q // 2, (q % 2) * CR

    def exchange(n, q):
        xp, base = where_q(q)
        rows = pl.ds(base, CR)
        return sent(
            0, f_buf.at[2, xp, :, rows], ybuf.at[n, xp, :, rows], x_s.at[n, q], x_r.at[n, q], other
        )

    def pair(ref, *at):
        *lead, rows = at
        return ref[(*lead, 0, rows)], ref[(*lead, 1, rows)]

    def put(ref, value, *at):
        *lead, rows = at
        ref[(*lead, 0, rows)] = value[0]
        ref[(*lead, 1, rows)] = value[1]

    def table(t, xp, rows, sign):
        re, im = pair(wg, t, xp, rows)
        return re, im if sign > 0 else -im

    def forward_chain(values, w, xp, rows):
        f = values[0]
        for k in range(1, 4):
            f = cadd(values[k], cmul(w, f))
            put(f_buf, f, k - 1, xp, rows)

    def first_pass(src, n, sign):
        for q in range(CHUNKS):
            xp, base = where_q(q)

            @pl.loop(0, CR // 8)
            def _(i):
                rows = pl.ds(pl.multiple_of(base + i * 8, 8), 8)
                forward_chain([pair(src, k, xp, rows) for k in range(4)], table(0, xp, rows, sign), xp, rows)

            exchange(n, q).start()

    def second_pass(src, n, sign, emit, acc):
        for q in range(CHUNKS):
            xp, base = where_q(q)
            exchange(n, q).wait()

            def step(i, acc):
                rows = pl.ds(pl.multiple_of(base + i * 8, 8), 8)
                w, g = table(0, xp, rows, sign), table(1, xp, rows, sign)
                t = pair(ybuf, n, xp, rows)
                out = [None] * 4
                for k in (3, 2, 1, 0):
                    u = cmul(w, t)
                    v = pair(src, k, xp, rows)
                    f = v if k == 0 else pair(f_buf, k - 1, xp, rows)
                    out[k] = cmul(g, cadd(f, u))
                    if k:
                        t = cadd(v, u)
                return emit(out, xp, rows, acc)

            acc = lax.fori_loop(0, CR // 8, step, acc)
            if emit.following is not None:
                exchange(emit.following, q).start()
        return acc

    zero = jnp.zeros((8, N), jnp.float32)

    def norm(acc, value):
        return acc + (value[0] * value[0] + value[1] * value[1])

    def reduce_start(n, rows):
        for i, tile in enumerate(rows):
            red_out[n, i] = tile
        copy = sent(0, red_out.at[n], red_in.at[n], rd_s.at[n], rd_r.at[n], other)
        copy.start()
        return copy

    def emit_first(out, xp, rows, acc):
        for k in range(4):
            put(w_buf, out[k], k, xp, rows)
        w = table(0, xp, rows, -1)
        forward_chain(out, w, xp, rows)
        return acc

    emit_first.following = 1

    def emit_back(out, xp, rows, acc):
        for k in range(4):
            put(s_buf, out[k], k, xp, rows)
        return acc

    emit_back.following = None

    first_pass(s_buf, 0, 1)
    second_pass(s_buf, 0, 1, emit_first, 0)

    @pl.loop(0, 4)
    def _(p):
        re, im = inverse_plane(load_from(w_buf, p), right, left)
        r_buf[p, 0] = re
        r_buf[p, 1] = im

    second_pass(w_buf, 1, -1, emit_back, 0)

    def gradient_step(p, acc):
        re, im = inverse_plane(load_from(s_buf, p), right, left)
        c = c4[p]
        re = r_buf[p, 0] - c * re
        im = r_buf[p, 1] - c * im
        g0[p, 0] = re
        g0[p, 1] = im
        acc = acc + tile_sum(re * re + im * im)
        forward_plane(c * re, c * im, right, left, store_to(s_buf, p))
        return acc

    zz0 = lax.fori_loop(0, 4, gradient_step, jnp.zeros((8, H), jnp.float32))

    sender = chip // 2
    send_index = 2 * chip + 1 + sender * (6 - 4 * chip)
    own_index = jnp.where(core == sender, 2 * chip + sender * (6 - 4 * chip), 4)

    def plane_copy(n, ref):
        return sent(0, ref.at[send_index], ref.at[4], pg_s.at[n], pg_r.at[n], other)

    def hat_copy(n, ref):
        return sent(0, ref.at[0], ref.at[4], ht_s.at[n], ht_r.at[n], other)

    first_pass(s_buf, 2, 1)

    @pl.when(core == sender)
    def _():
        plane_copy(0, g0).start()

    @pl.loop(0, 4)
    def _(p):
        forward_plane(g0[p, 0], g0[p, 1], right, left, store_to(gh0, p))

    @pl.when(core == 1)
    def _():
        hat_copy(0, gh0).start()

    def emit_image(out, xp, rows, acc):
        w = table(0, xp, rows, -1)
        image = []
        for k in range(4):
            m = csub(pair(gh0, k, xp, rows), out[k])
            acc = norm(acc, m)
            put(w_buf, m, k, xp, rows)
            image.append(m)
        forward_chain(image, w, xp, rows)
        return acc

    emit_image.following = 3
    mm0 = second_pass(s_buf, 2, 1, emit_image, zero)
    red0 = reduce_start(0, (zz0, tile_sum(mm0)))

    @pl.loop(0, 4)
    def _(p):
        re, im = inverse_plane(load_from(w_buf, p), right, left)
        r_buf[p, 0] = re
        r_buf[p, 1] = im

    second_pass(w_buf, 3, -1, emit_back, 0)
    red0.wait()
    zz_first = total_of(red_out[0, 0] + red_in[0, 0])
    mm_first = total_of(red_out[0, 1] + red_in[0, 1]) * (1.0 / (N * N))
    alpha0 = zz_first / mm_first

    def next_step(p, acc):
        re, im = inverse_plane(load_from(s_buf, p), right, left)
        c = c4[p]
        re = g0[p, 0] - alpha0 * (r_buf[p, 0] - c * re)
        im = g0[p, 1] - alpha0 * (r_buf[p, 1] - c * im)
        g1[p, 0] = re
        g1[p, 1] = im
        acc = acc + tile_sum(re * re + im * im)
        forward_plane(c * re, c * im, right, left, store_to(s_buf, p))
        return acc

    zz1 = lax.fori_loop(0, 4, next_step, jnp.zeros((8, H), jnp.float32))
    red1 = reduce_start(1, (zz1,))
    first_pass(s_buf, 4, 1)

    @pl.when(core == sender)
    def _():
        plane_copy(1, g1).start()

    @pl.loop(0, 4)
    def _(p):
        forward_plane(g1[p, 0], g1[p, 1], right, left, store_to(gh1, p))

    @pl.when(core == 1)
    def _():
        hat_copy(1, gh1).start()

    red1.wait()
    zz_second = total_of(red_out[1, 0] + red_in[1, 0])
    beta0 = zz_second / zz_first

    def emit_last(out, xp, rows, acc):
        for k in range(4):
            m = csub(pair(gh1, k, xp, rows), out[k])
            old = pair(w_buf, k, xp, rows)
            acc = norm(acc, (m[0] + beta0 * old[0], m[1] + beta0 * old[1]))
        return acc

    emit_last.following = None
    mm1 = second_pass(s_buf, 4, 1, emit_last, zero)
    red2 = reduce_start(2, (tile_sum(mm1),))

    @pl.when(core == sender)
    def _():
        plane_copy(0, g0).wait_send()
        plane_copy(1, g1).wait_send()

    @pl.when(core != sender)
    def _():
        plane_copy(0, g0).wait_recv()
        plane_copy(1, g1).wait_recv()

    @pl.when(core == 1)
    def _():
        hat_copy(0, gh0).wait_send()
        hat_copy(1, gh1).wait_send()

    @pl.when(core == 0)
    def _():
        hat_copy(0, gh0).wait_recv()
        hat_copy(1, gh1).wait_recv()

    load_h7.wait()
    inc_re, inc_im = incident(slab)
    red2.wait()
    mm_second = total_of(red_out[2, 0] + red_in[2, 0]) * (1.0 / (N * N))
    alpha1 = zz_second / mm_second
    weight0 = alpha0 + alpha1 * beta0

    hat = 4 * (1 - core)
    for xp in (0, 1):
        s7 = tuple(weight0 * gh0[hat, xp, i] + alpha1 * gh1[hat, xp, i] - mh[xp, i] for i in (0, 1))
        back = cmul((h7[xp, 0], h7[xp, 1]), s7)
        w_buf[0, xp, 0] = back[0]
        w_buf[0, xp, 1] = back[1]
    back_re, back_im = inverse_plane(load_from(w_buf, 0), right, left)
    more_re = weight0 * g0[own_index, 0] + alpha1 * g1[own_index, 0]
    more_im = weight0 * g0[own_index, 1] + alpha1 * g1[own_index, 1]
    sol_re = inc_re + more_re
    sol_im = inc_im + more_im
    fields[0] = sol_re
    fields[1] = sol_im
    part[...] = sol_re * back_re + sol_im * back_im

    for k in range(1, ILLUMS):
        peer = illum_peer(k)
        rows = pl.ds(pl.multiple_of(peer[0] * 8, 8), 8)
        sent(0, part.at[rows], rs_in.at[illum], rs_s, rs_r, peer).start()
    rs_in[illum] = part[my_rows, :]
    miss_re = more_re - meas[0]
    miss_im = more_im - meas[1]
    misfit_tile = tile_sum(miss_re * miss_re + miss_im * miss_im)
    is_last = jnp.where(slab == NZ - 1, 0.5, 0.0)
    misfit_row = is_last * jnp.sum(misfit_tile, axis=0, keepdims=True)
    wait_bytes(rs_in.at[pl.ds(0, ILLUMS - 1)], rs_s)
    wait_bytes(rs_in.at[pl.ds(0, ILLUMS - 1)], rs_r)

    rows = jnp.sum(rs_in[...], axis=0)
    square_row = jnp.sum(tile_sum(rows * rows), axis=0, keepdims=True)
    at = lax.broadcasted_iota(jnp.int32, (8, H), 0)
    ar_out[0] = jnp.where(at == 0, square_row, jnp.where(at == 1, misfit_row, 0.0))
    for k in range(1, NZ):
        sent(0, ar_out.at[0], ar1.at[slab], a1_s, a1_r, slab_peer(k)).start()
    ar1[slab] = ar_out[0]
    wait_bytes(ar1.at[pl.ds(0, NZ - 1)], a1_s)
    wait_bytes(ar1.at[pl.ds(0, NZ - 1)], a1_r)
    ar_out[1] = jnp.sum(ar1[...], axis=0)
    for k in range(1, ILLUMS):
        sent(0, ar_out.at[1], ar2.at[illum], a2_s, a2_r, illum_peer(k)).start()
    ar2[illum] = ar_out[1]
    wait_bytes(ar2.at[pl.ds(0, ILLUMS - 1)], a2_s)
    wait_bytes(ar2.at[pl.ds(0, ILLUMS - 1)], a2_r)
    sums = jnp.sum(ar2[...], axis=0)
    square = jnp.sum(sums[0:1], axis=1, keepdims=True)
    descent[...] = rows / jnp.sqrt(square * (1.0 / (NZ * N * N)) + 1e-06)
    misfit[0, 0] = jnp.sum(sums[1:2])


def body(angles, contrast, measured):
    right, left = dft_tables()
    wg, source = depth_tables()
    vmem = pl.BlockSpec(memory_space=pltpu.VMEM)
    smem = pl.BlockSpec(memory_space=pltpu.SMEM)
    anyspace = pl.BlockSpec(memory_space=pl.ANY)
    f32 = jnp.float32
    dma = pltpu.SemaphoreType.DMA
    spectral = (2, 2, H, N)
    fields, descent, misfit = pl.pallas_call(
        kernel,
        out_shape=(
            jax.ShapeDtypeStruct((2, N, N), f32),
            jax.ShapeDtypeStruct((8, N), f32),
            jax.ShapeDtypeStruct((1, 1), f32),
        ),
        in_specs=[smem, vmem, vmem, vmem, vmem, vmem, anyspace],
        out_specs=(vmem, vmem, smem),
        scratch_shapes=[
            pltpu.VMEM((N, N), f32),
            pltpu.VMEM((4, N, N), f32),
            pltpu.VMEM((4, *spectral), f32),
            pltpu.VMEM((3, *spectral), f32),
            pltpu.VMEM((4, *spectral), f32),
            pltpu.VMEM((5, *spectral), f32),
            pltpu.VMEM((5, *spectral), f32),
            pltpu.VMEM((5, 2, N, N), f32),
            pltpu.VMEM((5, 2, N, N), f32),
            pltpu.VMEM((4, 2, N, N), f32),
            pltpu.VMEM((5, *spectral), f32),
            pltpu.VMEM((3, 2, 8, H), f32),
            pltpu.VMEM((3, 2, 8, H), f32),
            pltpu.VMEM(spectral, f32),
            pltpu.VMEM(spectral, f32),
            pltpu.VMEM((N, N), f32),
            pltpu.VMEM((ILLUMS, 8, N), f32),
            pltpu.VMEM((2, 8, H), f32),
            pltpu.VMEM((NZ, 8, H), f32),
            pltpu.VMEM((ILLUMS, 8, H), f32),
            dma, dma, dma((4,)), dma((4,)),
            dma((5, CHUNKS)), dma((5, CHUNKS)),
            dma((3,)), dma((3,)), dma((2,)), dma((2,)), dma((2,)), dma((2,)), dma,
            dma, dma, dma, dma, dma, dma,
        ],
        compiler_params=pltpu.CompilerParams(
            collective_id=0, has_side_effects=True, vmem_limit_bytes=48 * 1024 * 1024
        ),
    )(
        angles, contrast.reshape(8, N), measured.reshape(2, N, N),
        jnp.asarray(right), jnp.asarray(left), jnp.asarray(wg), jnp.asarray(source),
    )
    return fields.reshape(1, 2, 1, N, N), descent.reshape(1, 8, N), misfit.reshape(())


def solution(mesh):
    return jax.shard_map(
        body,
        mesh=mesh,
        in_specs=(P("illum", None), P("slab", "illum", None), P("illum", None, None, None)),
        out_specs=(P("illum", None, "slab", None, None), P("slab", "illum", None), P()),
        check_vma=False,
    )
```

time: 727 us -> 99.8 us (0.14)
  blocking collectives: 264 us -> 0 us
  waiting for transfers between devices: 238 us -> 0 us
  Pallas kernels: 0 us -> 89.9 us
  other arithmetic: 77.6 us -> 0 us
  matrix products: 75.7 us -> 0 us
  starting transfers between devices: 31.9 us -> 0 us
  between operations: 23.3 us -> 2.47 us
    reduce_scatter x1 -> x0, waiting for transfers between devices: 204 us -> none  [body(): lax.psum_scatter(partial_value, 'illum', scatter_dimension=1, tiled=True)]
    psum x4 -> x0, blocking collectives: 121 us -> none  [the longest x1 79.9 us: body(): lax.psum((jnp.sum(gradient_rows * gradient_rows), misfit_local), ('illum'...]
    all_to_all x8 -> x0, blocking collectives: 102 us -> none  [the longest x5 63.5 us: convolve(): lax.all_to_all(spectral, 'slab', split_axis=2, concat_axis=1, tiled=True)]
    pallas_call x0 -> x1, Pallas kernels: none -> 89.9 us  [body(): pl.pallas_call(kernel, out_shape=(jax.ShapeDtypeStruct((2, N, N), f32), j...]
    dot_general x48 -> x0, matrix products: 75.7 us -> none  [the longest x24 38.4 us: fourier_transform(): jnp.einsum(einsum_form, values, sine_table, precision=highest_precision)]
    dot_general x6 -> x0, other arithmetic: 55.8 us -> none  [depth_sum(): jnp.einsum('zwxy,wxy->zxy', coupling_imaginary, imaginary_part, precision...]
    all_gather x1 -> x0, blocking collectives: 40.8 us -> none  [body(): contrast = lax.all_gather(contrast, 'illum', axis=1, tiled=True)]
    all_to_all x4 -> x0, waiting for transfers between devices: 33.8 us -> none  [the longest x3 24.6 us: convolve(): lax.all_to_all(column_list, 'slab', split_axis=1, concat_axis=2, tiled=True)]
  transfers between devices with their start and end apart: 5 -> 0, of which waited for: 5 -> 0; matrix products, arithmetic and copies ran while one was open for 1% -> 0% of each run, Pallas kernels for 0% -> 0%
where the time goes in v1:
time: 99.8 us; the launch traced here: 99.5 us
  Pallas kernels  89.9 us (90%)
  local copies, waits for them, and re-layouts  7.09 us (7%)
  between operations  2.47 us (2%)
    pallas_call x1, Pallas kernels, body(): pl.pallas_call(kernel, out_shape=(jax.ShapeDtypeStruct((2, N, N), f32), j...  89.9 us
    unnamed x14, local copies, waits for them, and re-layouts  7.09 us

profile of v1, /device:TPU:1, one launch (start us, length us, event | category | flops | bytes accessed | tf_op | source)
XLA Modules:
  0.0 99.5 jit_solution(14156770107584960378)
XLA Ops:
  0.6 0.0 copy-start
  0.6 1.2 %copy-done = f32[2,2,2,128,256]{4,3,2,1,0:T(8,128)S(1)} copy-done((f32[2,2,2,128,256]{4,3,2,1,0:T(8,128)S(1)}, f32[2,2,2,128,256]{4,3,2,1,0:T(8,128)}, u32[]{:S(2)}) %copy-start) | copy-done | bytes 1048600
  1.9 0.0 copy-start.1
  1.9 1.0 %copy-done.1 = f32[1,2,256,256]{3,2,1,0:T(8,128)S(1)} copy-done((f32[1,2,256,256]{3,2,1,0:T(8,128)S(1)}, f32[1,2,256,256]{3,2,1,0:T(8,128)}, u32[]{:S(2)}) %copy-start.1) | copy-done | bytes 524312
  2.9 0.0 copy-start.2
  2.9 1.0 %copy-done.2 = bf16[2,2,256,256]{3,2,1,0:T(8,128)(2,1)S(1)} copy-done((bf16[2,2,256,256]{3,2,1,0:T(8,128)(2,1)S(1)}, bf16[2,2,256,256]{3,2,1,0:T(8,128)(2,1)}, u32[]{:S(2)}) %copy-start.2) | copy-done | bytes 524312
  3.9 0.0 copy-start.3
  3.9 1.0 %copy-done.3 = bf16[2,2,256,256]{3,2,1,0:T(8,128)(2,1)S(1)} copy-done((bf16[2,2,256,256]{3,2,1,0:T(8,128)(2,1)S(1)}, bf16[2,2,256,256]{3,2,1,0:T(8,128)(2,1)}, u32[]{:S(2)}) %copy-start.3) | copy-done | bytes 524312
  5.0 0.0 copy-start.4
  5.0 0.7 copy-done.4
  5.7 0.0 copy-start.5
  5.7 0.7 copy-done.5
  6.3 89.9 %shard_map.94 = (f32[2,256,256]{2,1,0:T(8,128)S(1)}, f32[8,256]{1,0:T(8,128)S(1)}, f32[1,1]{1,0:T(1,128)}) custom-call(s32[1,2]{1,0:T(1,128)S(1)} %copy-done.5, f32[8,256]{1,0:T(8,128)S(1)} %bitcast.9, f32[2,256,256]{2,1,0:T(8,128)S(1)} %bitcast.8, bf16[2,2,256,256]{3,2,1,0:T(8,128)(2,1)S(1)} %copy-done.3, bf16[2,2,256,256]{3,2,1,0:T(8,128)(2,1)S(1)} %copy-done.2, ...), custom_call_target="tpu_custom_call" | custom-call | tf_op jit(solution)/shard_map/pallas_call | solution.py:556
  96.2 0.8 copy.14
  97.0 0.6 copy.15
Async XLA Ops:
  0.6 1.2 %copy-start = (f32[2,2,2,128,256]{4,3,2,1,0:T(8,128)S(1)}, f32[2,2,2,128,256]{4,3,2,1,0:T(8,128)}, u32[]{:S(2)}) copy-start(f32[2,2,2,128,256]{4,3,2,1,0:T(8,128)} %constant.10.clone.wg) | copy-start | bytes 3145732
  1.9 1.0 %copy-start.1 = (f32[1,2,256,256]{3,2,1,0:T(8,128)S(1)}, f32[1,2,256,256]{3,2,1,0:T(8,128)}, u32[]{:S(2)}) copy-start(f32[1,2,256,256]{3,2,1,0:T(8,128)} %param.9) | copy-start | bytes 1572868
  2.9 1.0 %copy-start.2 = (bf16[2,2,256,256]{3,2,1,0:T(8,128)(2,1)S(1)}, bf16[2,2,256,256]{3,2,1,0:T(8,128)(2,1)}, u32[]{:S(2)}) copy-start(bf16[2,2,256,256]{3,2,1,0:T(8,128)(2,1)} %constant.9.clone.left) | copy-start | bytes 1572868
  3.9 1.0 %copy-start.3 = (bf16[2,2,256,256]{3,2,1,0:T(8,128)(2,1)S(1)}, bf16[2,2,256,256]{3,2,1,0:T(8,128)(2,1)}, u32[]{:S(2)}) copy-start(bf16[2,2,256,256]{3,2,1,0:T(8,128)(2,1)} %constant.8.clone.right) | copy-start | bytes 1572868
  5.0 0.7 copy-start.4
  5.7 0.7 copy-start.5

commit v2 on v1

--- a/solution.py
+++ b/solution.py
@@ -3,7 +3,6 @@
 
 import jax
 import jax.numpy as jnp
-import ml_dtypes
 import numpy as np
 from jax import lax
 from jax.experimental import pallas as pl
@@ -22,10 +21,17 @@
 CR = 64
 
 
-def split_np(m):
-    hi = m.astype(ml_dtypes.bfloat16)
-    lo = (m - hi.astype(np.float64)).astype(ml_dtypes.bfloat16)
-    return np.stack([hi, lo])
+def far_first(a, b):
+    def length(step):
+        return min(step[0], a - step[0]) + min(step[1], b - step[1])
+
+    steps = [(i, j) for i in range(a) for j in range(b) if i or j]
+    return sorted(steps, key=length, reverse=True)
+
+
+ILLUM_STEPS = far_first(4, 8)
+CHIP_STEPS = far_first(4, 4)
+DEPTH_STEPS = sorted(range(1, 8), key=lambda k: -min(k, 8 - k))
 
 
 def dft_tables():
@@ -36,9 +42,7 @@
         theta = -2.0 * np.pi / N * ((n * (2 * m + q)) % N)
         c, s = np.cos(theta), np.sin(theta)
         out.append(np.block([[c, s], [-s, c]]))
-    right = np.stack([split_np(r) for r in out])
-    left = np.stack([split_np(np.ascontiguousarray(r.T)) for r in out])
-    return right, left
+    return np.stack(out + [r.T for r in out]).astype(np.float32)
 
 
 def depth_tables():
@@ -143,11 +147,11 @@
 
 
 def kernel(
-    angles, block, meas, right, left, wg, source_table,
+    angles_in, block, meas_in, dft_in, wg_in, source_table,
     fields, descent, misfit,
-    plane, c4, s_buf, f_buf, w_buf, gh0, gh1, g0, g1, r_buf, ybuf, red_out, red_in,
+    angles, meas, dft, right, left, wg, inc, zbuf, c4, s_buf, f_buf, w_buf, gh0, gh1, g0, g1, r_buf, ybuf, red_out, red_in,
     mh, h7, part, rs_in, ar_out, ar1, ar2,
-    ga_s, ga_r, gb_s, gb_r, x_s, x_r, rd_s, rd_r, pg_s, pg_r, ht_s, ht_r, h7_sem,
+    in_sem, ga_s, ga_r, gb_s, go_s, gb_r, x_s, x_r, rd_s, rd_r, pg_s, pg_r, ht_s, ht_r,
     rs_s, rs_r, a1_s, a1_r, a2_s, a2_r,
 ):
     illum = lax.axis_index("illum")
@@ -156,29 +160,62 @@
     core = slab - 2 * chip
     other = (illum, slab + 1 - 2 * core)
 
-    def illum_peer(k):
-        return (lax.rem(illum + k, ILLUMS), slab)
+    x, z = illum // 8, lax.rem(illum, 8)
+
+    def illum_at(dx, dz):
+        return lax.rem(x + dx, 4) * 8 + lax.rem(z + dz, 8)
 
     def slab_peer(k):
         return (illum, lax.rem(slab + k, NZ))
 
-    load_h7 = pltpu.make_async_copy(source_table.at[slab], h7, h7_sem)
-    load_h7.start()
+    def sent(src, dst, s_sem, r_sem, dev):
+        return pltpu.make_async_remote_copy(
+            src_ref=src, dst_ref=dst, send_sem=s_sem, recv_sem=r_sem, device_id=dev, device_id_type=MESH
+        )
+
+    def wait_bytes(ref, sem):
+        pltpu.make_async_copy(ref, ref, sem).wait()
 
     barrier = pltpu.get_barrier_semaphore()
-    for k in range(1, ILLUMS):
-        pl.semaphore_signal(barrier, inc=1, device_id=illum_peer(k), device_id_type=MESH)
+
+    def greet(peer):
+        pl.semaphore_signal(barrier, inc=1, device_id=peer, device_id_type=MESH)
+
+    for dx, dz in ILLUM_STEPS:
+        greet((illum_at(dx, dz), slab))
+    for dx in (2, 1, 3):
+        for k in range(4):
+            greet((illum_at(dx, 0), 4 * core + k))
     for k in range(1, NZ):
-        pl.semaphore_signal(barrier, inc=1, device_id=slab_peer(k), device_id_type=MESH)
-    pl.semaphore_wait(barrier, ILLUMS - 1 + NZ - 1)
-
-    my_rows = pl.ds(pl.multiple_of(illum * 8, 8), 8)
-    for k in range(1, ILLUMS):
-        pltpu.make_async_remote_copy(
-            src_ref=block, dst_ref=plane.at[my_rows], send_sem=ga_s, recv_sem=ga_r,
-            device_id=illum_peer(k), device_id_type=MESH,
-        ).start()
-    plane[my_rows, :] = block[...]
+        greet(slab_peer(k))
+
+    z_rows = pl.ds(pl.multiple_of(z * 8, 8), 8)
+    loads = [
+        pltpu.make_async_copy(src, dst, in_sem.at[i])
+        for i, (src, dst) in enumerate((
+            (block, zbuf.at[z_rows]), (angles_in, angles), (meas_in, meas), (dft_in, dft),
+            (wg_in, wg), (source_table.at[slab], h7),
+        ))
+    ]
+    for load in loads:
+        load.start()
+    for load in loads[:4]:
+        load.wait()
+    for q in (0, 1):
+        for i, value in enumerate(split(dft[q])):
+            right[q, i] = value
+        for i, value in enumerate(split(dft[2 + q])):
+            left[q, i] = value
+
+    def store_mh(q, value):
+        mh[q, 0] = value[:H]
+        mh[q, 1] = value[H:]
+
+    forward_plane(meas[0], meas[1], right, left, store_mh)
+    pl.semaphore_wait(barrier, ILLUMS - 1 + NZ - 1 + 12)
+
+    for dz in DEPTH_STEPS:
+        sent(zbuf.at[z_rows], zbuf.at[z_rows], ga_s, ga_r, (illum_at(0, dz), slab)).start()
 
     def angle_row(i):
         return jnp.sin(TILT * jnp.full((1, H), angles[0, i], jnp.int32).astype(jnp.float32))
@@ -207,57 +244,60 @@
     def load_from(ref, p):
         return lambda q: jnp.concatenate([ref[p, q, 0], ref[p, q, 1]], axis=0)
 
-    def store_mh(q, value):
-        mh[q, 0] = value[:H]
-        mh[q, 1] = value[H:]
-
-    forward_plane(meas[0], meas[1], right, left, store_mh)
-
-    def sent(n, src, dst, s_sem, r_sem, dev):
-        return pltpu.make_async_remote_copy(
-            src_ref=src, dst_ref=dst, send_sem=s_sem, recv_sem=r_sem, device_id=dev, device_id_type=MESH
-        )
-
-    def wait_bytes(ref, sem):
-        pltpu.make_async_copy(ref, ref, sem).wait()
-
-    wait_bytes(plane.at[pl.ds(0, (ILLUMS - 1) * 8)], ga_s)
-    wait_bytes(plane.at[pl.ds(0, (ILLUMS - 1) * 8)], ga_r)
+    def global_z(k):
+        return k + core * (7 - 2 * k)
+
+    def keep_incident(p):
+        inc[p, 0], inc[p, 1] = incident(global_z(p))
+
+    pl.loop(0, 4)(keep_incident)
+
+    wait_bytes(zbuf.at[pl.ds(0, 56)], ga_s)
+    wait_bytes(zbuf.at[pl.ds(0, 56)], ga_r)
 
     high = slab // 4
     slot = slab + high * (7 - 2 * slab)
-    for k in range(1, 4):
-        dest = 2 * lax.rem(chip + k, 4) + high
-        sent(0, plane, c4.at[slot], gb_s.at[k], gb_r.at[slot], (illum, dest)).start()
+    x_rows = pl.ds(pl.multiple_of(x * 64, 64), 64)
+    for dx, dy in CHIP_STEPS:
+        dest = 2 * lax.rem(chip + dy, 4) + high
+        sent(zbuf, c4.at[slot, x_rows], gb_s, gb_r.at[slot], (illum_at(dx, 0), dest)).start()
+
+    def to_other():
+        return sent(zbuf, c4.at[slot, x_rows], go_s, gb_r.at[slot], other)
 
     @pl.when(core != high)
     def _():
-        sent(0, plane, c4.at[slot], gb_s.at[0], gb_r.at[slot], other).start()
+        to_other().start()
 
     @pl.when(core == high)
     def _():
-        c4[slot] = plane[...]
-
-    for k in range(1, 4):
-        sent(0, plane, c4.at[slot], gb_s.at[k], gb_r.at[slot], other).wait_send()
+        c4[slot, x_rows] = zbuf[...]
+
+    def wait_plane(k):
+        here = (core == high) & (slot == k)
+
+        @pl.when(here)
+        def _():
+            wait_bytes(c4.at[k, pl.ds(0, 192)], gb_r.at[k])
+
+        @pl.when(jnp.logical_not(here))
+        def _():
+            wait_bytes(c4.at[k], gb_r.at[k])
+
+    for first in (0, 2):
+        wait_plane(first)
+        wait_plane(first + 1)
+        for p in (first, first + 1):
+            c = c4[p]
+            forward_plane(c * inc[p, 0], c * inc[p, 1], right, left, store_to(s_buf, p))
 
     @pl.when(core != high)
     def _():
-        sent(0, plane, c4.at[slot], gb_s.at[0], gb_r.at[slot], other).wait_send()
-
-    for k in range(4):
-        @pl.when((core != high) | (slot != k))
-        def _():
-            sent(0, plane, c4.at[k], gb_s.at[0], gb_r.at[k], other).wait_recv()
-
-    def global_z(k):
-        return k + core * (7 - 2 * k)
-
-    @pl.loop(0, 4)
-    def _(p):
-        re, im = incident(global_z(p))
-        c = c4[p]
-        forward_plane(c * re, c * im, right, left, store_to(s_buf, p))
+        to_other().wait_send()
+
+    for _ in range(15):
+        wait_bytes(zbuf, gb_s)
+    loads[4].wait()
 
     def where_q(q):
         return q // 2, (q % 2) * CR
@@ -266,7 +306,7 @@
         xp, base = where_q(q)
         rows = pl.ds(base, CR)
         return sent(
-            0, f_buf.at[2, xp, :, rows], ybuf.at[n, xp, :, rows], x_s.at[n, q], x_r.at[n, q], other
+            f_buf.at[2, xp, :, rows], ybuf.at[n, xp, :, rows], x_s.at[n, q], x_r.at[n, q], other
         )
 
     def pair(ref, *at):
@@ -331,7 +371,8 @@
     def reduce_start(n, rows):
         for i, tile in enumerate(rows):
             red_out[n, i] = tile
-        copy = sent(0, red_out.at[n], red_in.at[n], rd_s.at[n], rd_r.at[n], other)
+        used = pl.ds(0, len(rows))
+        copy = sent(red_out.at[n, used], red_in.at[n, used], rd_s.at[n], rd_r.at[n], other)
         copy.start()
         return copy
 
@@ -354,8 +395,7 @@
     first_pass(s_buf, 0, 1)
     second_pass(s_buf, 0, 1, emit_first, 0)
 
-    @pl.loop(0, 4)
-    def _(p):
+    for p in range(4):
         re, im = inverse_plane(load_from(w_buf, p), right, left)
         r_buf[p, 0] = re
         r_buf[p, 1] = im
@@ -373,17 +413,19 @@
         forward_plane(c * re, c * im, right, left, store_to(s_buf, p))
         return acc
 
-    zz0 = lax.fori_loop(0, 4, gradient_step, jnp.zeros((8, H), jnp.float32))
+    zz0 = jnp.zeros((8, H), jnp.float32)
+    for p in range(4):
+        zz0 = gradient_step(p, zz0)
 
     sender = chip // 2
     send_index = 2 * chip + 1 + sender * (6 - 4 * chip)
     own_index = jnp.where(core == sender, 2 * chip + sender * (6 - 4 * chip), 4)
 
     def plane_copy(n, ref):
-        return sent(0, ref.at[send_index], ref.at[4], pg_s.at[n], pg_r.at[n], other)
+        return sent(ref.at[send_index], ref.at[4], pg_s.at[n], pg_r.at[n], other)
 
     def hat_copy(n, ref):
-        return sent(0, ref.at[0], ref.at[4], ht_s.at[n], ht_r.at[n], other)
+        return sent(ref.at[0], ref.at[4], ht_s.at[n], ht_r.at[n], other)
 
     first_pass(s_buf, 2, 1)
 
@@ -391,8 +433,7 @@
     def _():
         plane_copy(0, g0).start()
 
-    @pl.loop(0, 4)
-    def _(p):
+    for p in range(4):
         forward_plane(g0[p, 0], g0[p, 1], right, left, store_to(gh0, p))
 
     @pl.when(core == 1)
@@ -414,8 +455,7 @@
     mm0 = second_pass(s_buf, 2, 1, emit_image, zero)
     red0 = reduce_start(0, (zz0, tile_sum(mm0)))
 
-    @pl.loop(0, 4)
-    def _(p):
+    for p in range(4):
         re, im = inverse_plane(load_from(w_buf, p), right, left)
         r_buf[p, 0] = re
         r_buf[p, 1] = im
@@ -437,7 +477,9 @@
         forward_plane(c * re, c * im, right, left, store_to(s_buf, p))
         return acc
 
-    zz1 = lax.fori_loop(0, 4, next_step, jnp.zeros((8, H), jnp.float32))
+    zz1 = jnp.zeros((8, H), jnp.float32)
+    for p in range(4):
+        zz1 = next_step(p, zz1)
     red1 = reduce_start(1, (zz1,))
     first_pass(s_buf, 4, 1)
 
@@ -445,8 +487,7 @@
     def _():
         plane_copy(1, g1).start()
 
-    @pl.loop(0, 4)
-    def _(p):
+    for p in range(4):
         forward_plane(g1[p, 0], g1[p, 1], right, left, store_to(gh1, p))
 
     @pl.when(core == 1)
@@ -488,7 +529,7 @@
         hat_copy(0, gh0).wait_recv()
         hat_copy(1, gh1).wait_recv()
 
-    load_h7.wait()
+    loads[5].wait()
     inc_re, inc_im = incident(slab)
     red2.wait()
     mm_second = total_of(red_out[2, 0] + red_in[2, 0]) * (1.0 / (N * N))
@@ -510,11 +551,11 @@
     fields[1] = sol_im
     part[...] = sol_re * back_re + sol_im * back_im
 
-    for k in range(1, ILLUMS):
-        peer = illum_peer(k)
-        rows = pl.ds(pl.multiple_of(peer[0] * 8, 8), 8)
-        sent(0, part.at[rows], rs_in.at[illum], rs_s, rs_r, peer).start()
-    rs_in[illum] = part[my_rows, :]
+    for dx, dz in ILLUM_STEPS:
+        peer = illum_at(dx, dz)
+        rows = pl.ds(pl.multiple_of(peer * 8, 8), 8)
+        sent(part.at[rows], rs_in.at[illum], rs_s, rs_r, (peer, slab)).start()
+    rs_in[illum] = part[pl.ds(pl.multiple_of(illum * 8, 8), 8), :]
     miss_re = more_re - meas[0]
     miss_im = more_im - meas[1]
     misfit_tile = tile_sum(miss_re * miss_re + miss_im * miss_im)
@@ -528,13 +569,13 @@
     at = lax.broadcasted_iota(jnp.int32, (8, H), 0)
     ar_out[0] = jnp.where(at == 0, square_row, jnp.where(at == 1, misfit_row, 0.0))
     for k in range(1, NZ):
-        sent(0, ar_out.at[0], ar1.at[slab], a1_s, a1_r, slab_peer(k)).start()
+        sent(ar_out.at[0], ar1.at[slab], a1_s, a1_r, slab_peer(k)).start()
     ar1[slab] = ar_out[0]
     wait_bytes(ar1.at[pl.ds(0, NZ - 1)], a1_s)
     wait_bytes(ar1.at[pl.ds(0, NZ - 1)], a1_r)
     ar_out[1] = jnp.sum(ar1[...], axis=0)
-    for k in range(1, ILLUMS):
-        sent(0, ar_out.at[1], ar2.at[illum], a2_s, a2_r, illum_peer(k)).start()
+    for dx, dz in ILLUM_STEPS:
+        sent(ar_out.at[1], ar2.at[illum], a2_s, a2_r, (illum_at(dx, dz), slab)).start()
     ar2[illum] = ar_out[1]
     wait_bytes(ar2.at[pl.ds(0, ILLUMS - 1)], a2_s)
     wait_bytes(ar2.at[pl.ds(0, ILLUMS - 1)], a2_r)
@@ -545,11 +586,11 @@
 
 
 def body(angles, contrast, measured):
-    right, left = dft_tables()
+    dft = dft_tables()
     wg, source = depth_tables()
     vmem = pl.BlockSpec(memory_space=pltpu.VMEM)
     smem = pl.BlockSpec(memory_space=pltpu.SMEM)
-    anyspace = pl.BlockSpec(memory_space=pl.ANY)
+    hbm = pl.BlockSpec(memory_space=pltpu.HBM)
     f32 = jnp.float32
     dma = pltpu.SemaphoreType.DMA
     spectral = (2, 2, H, N)
@@ -560,10 +601,17 @@
             jax.ShapeDtypeStruct((8, N), f32),
             jax.ShapeDtypeStruct((1, 1), f32),
         ),
-        in_specs=[smem, vmem, vmem, vmem, vmem, vmem, anyspace],
+        in_specs=[hbm] * 6,
         out_specs=(vmem, vmem, smem),
         scratch_shapes=[
-            pltpu.VMEM((N, N), f32),
+            pltpu.SMEM((1, 2), jnp.int32),
+            pltpu.VMEM((2, N, N), f32),
+            pltpu.VMEM((4, N, N), f32),
+            pltpu.VMEM((2, 2, N, N), jnp.bfloat16),
+            pltpu.VMEM((2, 2, N, N), jnp.bfloat16),
+            pltpu.VMEM((2, *spectral), f32),
+            pltpu.VMEM((4, 2, N, N), f32),
+            pltpu.VMEM((64, N), f32),
             pltpu.VMEM((4, N, N), f32),
             pltpu.VMEM((4, *spectral), f32),
             pltpu.VMEM((3, *spectral), f32),
@@ -583,17 +631,17 @@
             pltpu.VMEM((2, 8, H), f32),
             pltpu.VMEM((NZ, 8, H), f32),
             pltpu.VMEM((ILLUMS, 8, H), f32),
-            dma, dma, dma((4,)), dma((4,)),
+            dma((6,)), dma, dma, dma, dma, dma((4,)),
             dma((5, CHUNKS)), dma((5, CHUNKS)),
-            dma((3,)), dma((3,)), dma((2,)), dma((2,)), dma((2,)), dma((2,)), dma,
+            dma((3,)), dma((3,)), dma((2,)), dma((2,)), dma((2,)), dma((2,)),
             dma, dma, dma, dma, dma, dma,
         ],
         compiler_params=pltpu.CompilerParams(
-            collective_id=0, has_side_effects=True, vmem_limit_bytes=48 * 1024 * 1024
+            collective_id=0, has_side_effects=True, vmem_limit_bytes=53 * 1024 * 1024,
         ),
     )(
         angles, contrast.reshape(8, N), measured.reshape(2, N, N),
-        jnp.asarray(right), jnp.asarray(left), jnp.asarray(wg), jnp.asarray(source),
+        jnp.asarray(dft), jnp.asarray(wg), jnp.asarray(source),
     )
     return fields.reshape(1, 2, 1, N, N), descent.reshape(1, 8, N), misfit.reshape(())
 

time: 99.8 us -> 85.2 us (0.85)
  Pallas kernels: 89.9 us -> 79.9 us
  local copies, waits for them, and re-layouts: 7.09 us -> 2.74 us
    pallas_call x1, Pallas kernels: 89.9 us -> 79.9 us  [body(): pl.pallas_call(kernel, out_shape=(jax.ShapeDtypeStruct((2, N, N), f32), j...]
    unnamed x14 -> x6, local copies, waits for them, and re-layouts: 7.09 us -> 2.74 us
where the time goes in v2:
time: 85.2 us; the launch traced here: 85.1 us
  Pallas kernels  79.9 us (94%)
  local copies, waits for them, and re-layouts  2.74 us (3%)
  between operations  2.41 us (3%)
    pallas_call x1, Pallas kernels, body(): pl.pallas_call(kernel, out_shape=(jax.ShapeDtypeStruct((2, N, N), f32), j...  79.9 us
    unnamed x6, local copies, waits for them, and re-layouts  2.74 us

profile of v2, /device:TPU:1, one launch (start us, length us, event | category | flops | bytes accessed | tf_op | source)
XLA Modules:
  0.0 85.1 jit_solution(3587680273450894053)
XLA Ops:
  0.6 0.0 copy-start
  0.6 0.7 copy-done
  1.3 0.0 copy-start.1
  1.3 0.7 copy-done.1
  2.0 79.9 %shard_map.85 = (f32[2,256,256]{2,1,0:T(8,128)S(1)}, f32[8,256]{1,0:T(8,128)S(1)}, f32[1,1]{1,0:T(1,128)}) custom-call(s32[1,2]{1,0:T(1,128)S(1)} %copy-done.1, f32[8,256]{1,0:T(8,128)S(1)} %bitcast.8, f32[2,256,256]{2,1,0:T(8,128)} %bitcast.10, f32[4,256,256]{2,1,0:T(8,128)} %constant.6.clone.dft_in, f32[2,2,2,128,256]{4,3,2,1,0:T(8,128)} %constant.7.clone.wg_in, ...), custom_call_target="tpu_custom_call" | custom-call | tf_op jit(solution)/shard_map/pallas_call | solution.py:597
  81.9 0.8 copy.13
  82.7 0.6 copy.14
Async XLA Ops:
  0.6 0.7 copy-start
  1.3 0.7 copy-start.1

commit v3 on v2

--- a/solution.py
+++ b/solution.py
@@ -1,4 +1,4 @@
-import functools
+import itertools
 import math
 
 import jax
@@ -17,20 +17,20 @@
 WAVE = 2.0 * math.pi / 8.0
 DAMPING = 0.2
 TILT = 0.04
-CHUNKS = 4
-CR = 64
-
-
-def far_first(a, b):
+
+
+def far_first(*sizes):
     def length(step):
-        return min(step[0], a - step[0]) + min(step[1], b - step[1])
-
-    steps = [(i, j) for i in range(a) for j in range(b) if i or j]
+        return sum(min(k, n - k) for k, n in zip(step, sizes))
+
+    steps = [step for step in itertools.product(*map(range, sizes)) if any(step)]
     return sorted(steps, key=length, reverse=True)
 
 
 ILLUM_STEPS = far_first(4, 8)
-CHIP_STEPS = far_first(4, 4)
+CHIP_STEPS = [(dx, dy) for dy in (2, 0, 1, 3) for dx in (2, 1, 3, 0) if dx or dy]
+ALL_STEPS = far_first(4, 8, 4)
+CHIPS = 128
 DEPTH_STEPS = sorted(range(1, 8), key=lambda k: -min(k, 8 - k))
 
 
@@ -71,7 +71,11 @@
     return hi, lo
 
 
-def dot_right(a, m_ref, q):
+def dot_right(a, m_ref, q, exact=True):
+    if not exact:
+        hi = a.astype(jnp.bfloat16)
+        m = jnp.concatenate([m_ref[q, 0], m_ref[q, 1]], axis=0)
+        return jnp.dot(jnp.concatenate([hi, hi], axis=1), m, preferred_element_type=jnp.float32)
     hi, lo = split(a)
     mh, ml = m_ref[q, 0], m_ref[q, 1]
     return jnp.dot(
@@ -81,7 +85,11 @@
     )
 
 
-def dot_left(m_ref, q, a):
+def dot_left(m_ref, q, a, exact=True):
+    if not exact:
+        hi = a.astype(jnp.bfloat16)
+        m = jnp.concatenate([m_ref[q, 0], m_ref[q, 1]], axis=1)
+        return jnp.dot(m, jnp.concatenate([hi, hi], axis=0), preferred_element_type=jnp.float32)
     hi, lo = split(a)
     mh, ml = m_ref[q, 0], m_ref[q, 1]
     return jnp.dot(
@@ -91,20 +99,20 @@
     )
 
 
-def forward_plane(re, im, right, left, store):
+def forward_plane(re, im, right, left, store, exact=True):
     halves = []
     for q in (0, 1):
         if q == 0:
             a = jnp.concatenate([re[:, :H] + re[:, H:], im[:, :H] + im[:, H:]], axis=1)
         else:
             a = jnp.concatenate([re[:, :H] - re[:, H:], im[:, :H] - im[:, H:]], axis=1)
-        halves.append(dot_right(a, right, q))
+        halves.append(dot_right(a, right, q, exact))
     for q in (0, 1):
         parts = []
         for t in halves:
             u = t[:H] + t[H:] if q == 0 else t[:H] - t[H:]
             parts.append(jnp.concatenate([u[:, :H], u[:, H:]], axis=0))
-        store(q, dot_left(left, q, jnp.concatenate(parts, axis=1)))
+        store(q, dot_left(left, q, jnp.concatenate(parts, axis=1), exact))
 
 
 def inverse_plane(load, right, left):
@@ -150,7 +158,7 @@
     angles_in, block, meas_in, dft_in, wg_in, source_table,
     fields, descent, misfit,
     angles, meas, dft, right, left, wg, inc, zbuf, c4, s_buf, f_buf, w_buf, gh0, gh1, g0, g1, r_buf, ybuf, red_out, red_in,
-    mh, h7, part, rs_in, ar_out, ar1, ar2,
+    mh, h7, part, rs_in, ar_out, ar_in,
     in_sem, ga_s, ga_r, gb_s, go_s, gb_r, x_s, x_r, rd_s, rd_r, pg_s, pg_r, ht_s, ht_r,
     rs_s, rs_r, a1_s, a1_r, a2_s, a2_r,
 ):
@@ -181,8 +189,8 @@
     def greet(peer):
         pl.semaphore_signal(barrier, inc=1, device_id=peer, device_id_type=MESH)
 
-    for dx, dz in ILLUM_STEPS:
-        greet((illum_at(dx, dz), slab))
+    for dz in DEPTH_STEPS:
+        greet((illum_at(0, dz), slab))
     for dx in (2, 1, 3):
         for k in range(4):
             greet((illum_at(dx, 0), 4 * core + k))
@@ -212,7 +220,7 @@
         mh[q, 1] = value[H:]
 
     forward_plane(meas[0], meas[1], right, left, store_mh)
-    pl.semaphore_wait(barrier, ILLUMS - 1 + NZ - 1 + 12)
+    pl.semaphore_wait(barrier, 7 + 12 + 7)
 
     for dz in DEPTH_STEPS:
         sent(zbuf.at[z_rows], zbuf.at[z_rows], ga_s, ga_r, (illum_at(0, dz), slab)).start()
@@ -252,7 +260,6 @@
 
     pl.loop(0, 4)(keep_incident)
 
-    wait_bytes(zbuf.at[pl.ds(0, 56)], ga_s)
     wait_bytes(zbuf.at[pl.ds(0, 56)], ga_r)
 
     high = slab // 4
@@ -284,84 +291,92 @@
         def _():
             wait_bytes(c4.at[k], gb_r.at[k])
 
-    for first in (0, 2):
-        wait_plane(first)
-        wait_plane(first + 1)
-        for p in (first, first + 1):
-            c = c4[p]
-            forward_plane(c * inc[p, 0], c * inc[p, 1], right, left, store_to(s_buf, p))
-
-    @pl.when(core != high)
-    def _():
-        to_other().wait_send()
-
-    for _ in range(15):
-        wait_bytes(zbuf, gb_s)
+    everything = slice(None)
+
+    def pair(ref, *at, rows=everything):
+        return ref[(*at, 0, rows)], ref[(*at, 1, rows)]
+
+    def put(ref, value, *at, rows=everything):
+        ref[(*at, 0, rows)] = value[0]
+        ref[(*at, 1, rows)] = value[1]
+
+    def table(t, xp, sign, rows=everything):
+        re, im = pair(wg, t, xp, rows=rows)
+        return re, im if sign > 0 else -im
+
+    def exchange(n, xp):
+        return sent(f_buf.at[2, xp], ybuf.at[n, xp], x_s.at[n, xp], x_r.at[n, xp], other)
+
+    def forward_chained(p, re, im, n, exact=True):
+        def store(q, value):
+            v = value[:H], value[H:]
+            put(s_buf, v, p, q)
+            if p:
+                before = pair(s_buf, 0, q) if p == 1 else pair(f_buf, p - 2, q)
+                put(f_buf, cadd(v, cmul(table(0, q, 1), before)), p - 1, q)
+            if p == 3:
+                exchange(n, q).start()
+
+        forward_plane(re, im, right, left, store, exact)
+
+    first = 2 * lax.rem(chip + core, 2)
+    for i in range(4):
+        p = lax.rem(first + i, 4)
+        wait_plane(p)
+        c = c4[p]
+        forward_plane(c * inc[p, 0], c * inc[p, 1], right, left, store_to(s_buf, p))
     loads[4].wait()
-
-    def where_q(q):
-        return q // 2, (q % 2) * CR
-
-    def exchange(n, q):
-        xp, base = where_q(q)
-        rows = pl.ds(base, CR)
-        return sent(
-            f_buf.at[2, xp, :, rows], ybuf.at[n, xp, :, rows], x_s.at[n, q], x_r.at[n, q], other
-        )
-
-    def pair(ref, *at):
-        *lead, rows = at
-        return ref[(*lead, 0, rows)], ref[(*lead, 1, rows)]
-
-    def put(ref, value, *at):
-        *lead, rows = at
-        ref[(*lead, 0, rows)] = value[0]
-        ref[(*lead, 1, rows)] = value[1]
-
-    def table(t, xp, rows, sign):
-        re, im = pair(wg, t, xp, rows)
-        return re, im if sign > 0 else -im
-
-    def forward_chain(values, w, xp, rows):
-        f = values[0]
-        for k in range(1, 4):
-            f = cadd(values[k], cmul(w, f))
-            put(f_buf, f, k - 1, xp, rows)
-
-    def first_pass(src, n, sign):
-        for q in range(CHUNKS):
-            xp, base = where_q(q)
-
-            @pl.loop(0, CR // 8)
-            def _(i):
-                rows = pl.ds(pl.multiple_of(base + i * 8, 8), 8)
-                forward_chain([pair(src, k, xp, rows) for k in range(4)], table(0, xp, rows, sign), xp, rows)
-
-            exchange(n, q).start()
+    for xp in (0, 1):
+
+        @pl.loop(0, H // 8)
+        def _(i):
+            rows = pl.ds(pl.multiple_of(i * 8, 8), 8)
+            w = table(0, xp, 1, rows)
+            f = pair(s_buf, 0, xp, rows=rows)
+            for k in range(1, 4):
+                f = cadd(pair(s_buf, k, xp, rows=rows), cmul(w, f))
+                put(f_buf, f, k - 1, xp, rows=rows)
+
+        exchange(0, xp).start()
+    fields[0], fields[1] = incident(slab)
 
     def second_pass(src, n, sign, emit, acc):
-        for q in range(CHUNKS):
-            xp, base = where_q(q)
-            exchange(n, q).wait()
+        for xp in (0, 1):
+            exchange(n, xp).wait()
 
             def step(i, acc):
-                rows = pl.ds(pl.multiple_of(base + i * 8, 8), 8)
-                w, g = table(0, xp, rows, sign), table(1, xp, rows, sign)
-                t = pair(ybuf, n, xp, rows)
+                rows = pl.ds(pl.multiple_of(i * 8, 8), 8)
+                w, g = table(0, xp, sign, rows), table(1, xp, sign, rows)
+                t = pair(ybuf, n, xp, rows=rows)
                 out = [None] * 4
                 for k in (3, 2, 1, 0):
                     u = cmul(w, t)
-                    v = pair(src, k, xp, rows)
-                    f = v if k == 0 else pair(f_buf, k - 1, xp, rows)
+                    v = pair(src, k, xp, rows=rows)
+                    f = v if k == 0 else pair(f_buf, k - 1, xp, rows=rows)
                     out[k] = cmul(g, cadd(f, u))
                     if k:
                         t = cadd(v, u)
                 return emit(out, xp, rows, acc)
 
-            acc = lax.fori_loop(0, CR // 8, step, acc)
+            acc = lax.fori_loop(0, H // 8, step, acc)
             if emit.following is not None:
-                exchange(emit.following, q).start()
+                exchange(emit.following, xp).start()
         return acc
+
+    def inverse_back(src, n, keep):
+        for xp in (0, 1):
+            exchange(n, xp).wait()
+        for p in (3, 2, 1, 0):
+
+            def load(q):
+                u = cmul(table(0, q, -1), pair(ybuf, n, q))
+                v = pair(src, p, q)
+                f = v if p == 0 else pair(f_buf, p - 1, q)
+                if p:
+                    put(ybuf, cadd(v, u), n, q)
+                return jnp.concatenate(cmul(table(1, q, -1), cadd(f, u)), axis=0)
+
+            keep(p, *inverse_plane(load, right, left))
 
     zero = jnp.zeros((8, N), jnp.float32)
 
@@ -376,23 +391,20 @@
         copy.start()
         return copy
 
+    def forward_chain(values, w, xp, rows):
+        f = values[0]
+        for k in range(1, 4):
+            f = cadd(values[k], cmul(w, f))
+            put(f_buf, f, k - 1, xp, rows=rows)
+
     def emit_first(out, xp, rows, acc):
         for k in range(4):
-            put(w_buf, out[k], k, xp, rows)
-        w = table(0, xp, rows, -1)
-        forward_chain(out, w, xp, rows)
+            put(w_buf, out[k], k, xp, rows=rows)
+        forward_chain(out, table(0, xp, -1, rows), xp, rows)
         return acc
 
     emit_first.following = 1
 
-    def emit_back(out, xp, rows, acc):
-        for k in range(4):
-            put(s_buf, out[k], k, xp, rows)
-        return acc
-
-    emit_back.following = None
-
-    first_pass(s_buf, 0, 1)
     second_pass(s_buf, 0, 1, emit_first, 0)
 
     for p in range(4):
@@ -400,22 +412,21 @@
         r_buf[p, 0] = re
         r_buf[p, 1] = im
 
-    second_pass(w_buf, 1, -1, emit_back, 0)
-
-    def gradient_step(p, acc):
-        re, im = inverse_plane(load_from(s_buf, p), right, left)
+    square_sums = []
+
+    def keep_gradient(p, re, im):
         c = c4[p]
         re = r_buf[p, 0] - c * re
         im = r_buf[p, 1] - c * im
         g0[p, 0] = re
         g0[p, 1] = im
-        acc = acc + tile_sum(re * re + im * im)
-        forward_plane(c * re, c * im, right, left, store_to(s_buf, p))
-        return acc
-
-    zz0 = jnp.zeros((8, H), jnp.float32)
+        square_sums.append(tile_sum(re * re + im * im))
+
+    inverse_back(w_buf, 1, keep_gradient)
+    zz0 = sum(square_sums)
     for p in range(4):
-        zz0 = gradient_step(p, zz0)
+        c = c4[p]
+        forward_chained(p, c * g0[p, 0], c * g0[p, 1], 2)
 
     sender = chip // 2
     send_index = 2 * chip + 1 + sender * (6 - 4 * chip)
@@ -424,10 +435,11 @@
     def plane_copy(n, ref):
         return sent(ref.at[send_index], ref.at[4], pg_s.at[n], pg_r.at[n], other)
 
-    def hat_copy(n, ref):
-        return sent(ref.at[0], ref.at[4], ht_s.at[n], ht_r.at[n], other)
-
-    first_pass(s_buf, 2, 1)
+    def hat_copy():
+        return sent(gh0.at[0], gh0.at[4], ht_s.at[0], ht_r.at[0], other)
+
+    def last_copy():
+        return sent(g1.at[0], g1.at[5], ht_s.at[1], ht_r.at[1], other)
 
     @pl.when(core == sender)
     def _():
@@ -438,17 +450,16 @@
 
     @pl.when(core == 1)
     def _():
-        hat_copy(0, gh0).start()
+        hat_copy().start()
 
     def emit_image(out, xp, rows, acc):
-        w = table(0, xp, rows, -1)
         image = []
         for k in range(4):
-            m = csub(pair(gh0, k, xp, rows), out[k])
+            m = csub(pair(gh0, k, xp, rows=rows), out[k])
             acc = norm(acc, m)
-            put(w_buf, m, k, xp, rows)
+            put(w_buf, m, k, xp, rows=rows)
             image.append(m)
-        forward_chain(image, w, xp, rows)
+        forward_chain(image, table(0, xp, -1, rows), xp, rows)
         return acc
 
     emit_image.following = 3
@@ -460,39 +471,37 @@
         r_buf[p, 0] = re
         r_buf[p, 1] = im
 
-    second_pass(w_buf, 3, -1, emit_back, 0)
     red0.wait()
     zz_first = total_of(red_out[0, 0] + red_in[0, 0])
     mm_first = total_of(red_out[0, 1] + red_in[0, 1]) * (1.0 / (N * N))
     alpha0 = zz_first / mm_first
 
-    def next_step(p, acc):
-        re, im = inverse_plane(load_from(s_buf, p), right, left)
+    square_sums = []
+
+    def keep_next(p, re, im):
         c = c4[p]
         re = g0[p, 0] - alpha0 * (r_buf[p, 0] - c * re)
         im = g0[p, 1] - alpha0 * (r_buf[p, 1] - c * im)
         g1[p, 0] = re
         g1[p, 1] = im
-        acc = acc + tile_sum(re * re + im * im)
-        forward_plane(c * re, c * im, right, left, store_to(s_buf, p))
-        return acc
-
-    zz1 = jnp.zeros((8, H), jnp.float32)
+        square_sums.append(tile_sum(re * re + im * im))
+
+    inverse_back(w_buf, 3, keep_next)
+    red1 = reduce_start(1, (sum(square_sums),))
     for p in range(4):
-        zz1 = next_step(p, zz1)
-    red1 = reduce_start(1, (zz1,))
-    first_pass(s_buf, 4, 1)
+        c = c4[p]
+        forward_chained(p, c * g1[p, 0], c * g1[p, 1], 4, exact=False)
 
     @pl.when(core == sender)
     def _():
         plane_copy(1, g1).start()
 
     for p in range(4):
-        forward_plane(g1[p, 0], g1[p, 1], right, left, store_to(gh1, p))
+        forward_plane(g1[p, 0], g1[p, 1], right, left, store_to(gh1, p), exact=False)
 
     @pl.when(core == 1)
     def _():
-        hat_copy(1, gh1).start()
+        last_copy().start()
 
     red1.wait()
     zz_second = total_of(red_out[1, 0] + red_in[1, 0])
@@ -500,8 +509,8 @@
 
     def emit_last(out, xp, rows, acc):
         for k in range(4):
-            m = csub(pair(gh1, k, xp, rows), out[k])
-            old = pair(w_buf, k, xp, rows)
+            m = csub(pair(gh1, k, xp, rows=rows), out[k])
+            old = pair(w_buf, k, xp, rows=rows)
             acc = norm(acc, (m[0] + beta0 * old[0], m[1] + beta0 * old[1]))
         return acc
 
@@ -521,16 +530,17 @@
 
     @pl.when(core == 1)
     def _():
-        hat_copy(0, gh0).wait_send()
-        hat_copy(1, gh1).wait_send()
+        hat_copy().wait_send()
+        last_copy().wait_send()
 
     @pl.when(core == 0)
     def _():
-        hat_copy(0, gh0).wait_recv()
-        hat_copy(1, gh1).wait_recv()
+        hat_copy().wait_recv()
+        last_copy().wait_recv()
 
     loads[5].wait()
-    inc_re, inc_im = incident(slab)
+    last = 5 * (1 - core)
+    forward_plane(g1[last, 0], g1[last, 1], right, left, store_to(gh1, 4))
     red2.wait()
     mm_second = total_of(red_out[2, 0] + red_in[2, 0]) * (1.0 / (N * N))
     alpha1 = zz_second / mm_second
@@ -538,15 +548,15 @@
 
     hat = 4 * (1 - core)
     for xp in (0, 1):
-        s7 = tuple(weight0 * gh0[hat, xp, i] + alpha1 * gh1[hat, xp, i] - mh[xp, i] for i in (0, 1))
+        s7 = tuple(weight0 * gh0[hat, xp, i] + alpha1 * gh1[4, xp, i] - mh[xp, i] for i in (0, 1))
         back = cmul((h7[xp, 0], h7[xp, 1]), s7)
         w_buf[0, xp, 0] = back[0]
         w_buf[0, xp, 1] = back[1]
     back_re, back_im = inverse_plane(load_from(w_buf, 0), right, left)
     more_re = weight0 * g0[own_index, 0] + alpha1 * g1[own_index, 0]
     more_im = weight0 * g0[own_index, 1] + alpha1 * g1[own_index, 1]
-    sol_re = inc_re + more_re
-    sol_im = inc_im + more_im
+    sol_re = fields[0] + more_re
+    sol_im = fields[1] + more_im
     fields[0] = sol_re
     fields[1] = sol_im
     part[...] = sol_re * back_re + sol_im * back_im
@@ -561,28 +571,43 @@
     misfit_tile = tile_sum(miss_re * miss_re + miss_im * miss_im)
     is_last = jnp.where(slab == NZ - 1, 0.5, 0.0)
     misfit_row = is_last * jnp.sum(misfit_tile, axis=0, keepdims=True)
-    wait_bytes(rs_in.at[pl.ds(0, ILLUMS - 1)], rs_s)
     wait_bytes(rs_in.at[pl.ds(0, ILLUMS - 1)], rs_r)
 
     rows = jnp.sum(rs_in[...], axis=0)
     square_row = jnp.sum(tile_sum(rows * rows), axis=0, keepdims=True)
-    at = lax.broadcasted_iota(jnp.int32, (8, H), 0)
-    ar_out[0] = jnp.where(at == 0, square_row, jnp.where(at == 1, misfit_row, 0.0))
-    for k in range(1, NZ):
-        sent(ar_out.at[0], ar1.at[slab], a1_s, a1_r, slab_peer(k)).start()
-    ar1[slab] = ar_out[0]
-    wait_bytes(ar1.at[pl.ds(0, NZ - 1)], a1_s)
-    wait_bytes(ar1.at[pl.ds(0, NZ - 1)], a1_r)
-    ar_out[1] = jnp.sum(ar1[...], axis=0)
-    for dx, dz in ILLUM_STEPS:
-        sent(ar_out.at[1], ar2.at[illum], a2_s, a2_r, (illum_at(dx, dz), slab)).start()
-    ar2[illum] = ar_out[1]
-    wait_bytes(ar2.at[pl.ds(0, ILLUMS - 1)], a2_s)
-    wait_bytes(ar2.at[pl.ds(0, ILLUMS - 1)], a2_r)
-    sums = jnp.sum(ar2[...], axis=0)
-    square = jnp.sum(sums[0:1], axis=1, keepdims=True)
+    lane = lax.broadcasted_iota(jnp.int32, (1, H), 1)
+    both = jnp.where(
+        lane < H // 2,
+        square_row + pltpu.roll(square_row, H // 2, 1),
+        misfit_row + pltpu.roll(misfit_row, H // 2, 1),
+    )
+    ar_out[0] = both
+    pair_sum = sent(ar_out.at[0], ar_out.at[1], a1_s, a1_r, other)
+    pair_sum.start()
+    pair_sum.wait_recv()
+    ar_out[2] = both + ar_out[1]
+    me = illum * 4 + chip
+    for dx, dz, dy in ALL_STEPS:
+        peer = (illum_at(dx, dz), 2 * lax.rem(chip + dy, 4) + core)
+        sent(ar_out.at[2], ar_in.at[me], a2_s, a2_r, peer).start()
+    ar_in[me] = ar_out[2]
+    wait_bytes(ar_in.at[pl.ds(0, CHIPS - 1)], a2_r)
+    sums = jnp.sum(ar_in[...], axis=0)
+    square = jnp.sum(jnp.where(lane < H // 2, sums, 0.0), axis=1, keepdims=True)
     descent[...] = rows / jnp.sqrt(square * (1.0 / (NZ * N * N)) + 1e-06)
-    misfit[0, 0] = jnp.sum(sums[1:2])
+    misfit[0, 0] = jnp.sum(jnp.where(lane < H // 2, 0.0, sums))
+
+    wait_bytes(zbuf.at[pl.ds(0, 56)], ga_s)
+
+    @pl.when(core != high)
+    def _():
+        to_other().wait_send()
+
+    for _ in range(15):
+        wait_bytes(zbuf, gb_s)
+    wait_bytes(rs_in.at[pl.ds(0, ILLUMS - 1)], rs_s)
+    pair_sum.wait_send()
+    wait_bytes(ar_in.at[pl.ds(0, CHIPS - 1)], a2_s)
 
 
 def body(angles, contrast, measured):
@@ -619,7 +644,7 @@
             pltpu.VMEM((5, *spectral), f32),
             pltpu.VMEM((5, *spectral), f32),
             pltpu.VMEM((5, 2, N, N), f32),
-            pltpu.VMEM((5, 2, N, N), f32),
+            pltpu.VMEM((6, 2, N, N), f32),
             pltpu.VMEM((4, 2, N, N), f32),
             pltpu.VMEM((5, *spectral), f32),
             pltpu.VMEM((3, 2, 8, H), f32),
@@ -628,11 +653,10 @@
             pltpu.VMEM(spectral, f32),
             pltpu.VMEM((N, N), f32),
             pltpu.VMEM((ILLUMS, 8, N), f32),
-            pltpu.VMEM((2, 8, H), f32),
-            pltpu.VMEM((NZ, 8, H), f32),
-            pltpu.VMEM((ILLUMS, 8, H), f32),
+            pltpu.VMEM((3, 1, H), f32),
+            pltpu.VMEM((CHIPS, 1, H), f32),
             dma((6,)), dma, dma, dma, dma, dma((4,)),
-            dma((5, CHUNKS)), dma((5, CHUNKS)),
+            dma((5, 2)), dma((5, 2)),
             dma((3,)), dma((3,)), dma((2,)), dma((2,)), dma((2,)), dma((2,)),
             dma, dma, dma, dma, dma, dma,
         ],

time: 85.2 us -> 81.5 us (0.957)
  Pallas kernels: 79.9 us -> 76.2 us
    pallas_call x1, Pallas kernels: 79.9 us -> 76.2 us  [body(): pl.pallas_call(kernel, out_shape=(jax.ShapeDtypeStruct((2, N, N), f32), j...]
where the time goes in v3:
time: 81.5 us; the launch traced here: 81.3 us
  Pallas kernels  76.2 us (93%)
  local copies, waits for them, and re-layouts  2.74 us (3%)
  between operations  2.41 us (3%)
    pallas_call x1, Pallas kernels, body(): pl.pallas_call(kernel, out_shape=(jax.ShapeDtypeStruct((2, N, N), f32), j...  76.2 us
    unnamed x6, local copies, waits for them, and re-layouts  2.74 us

profile of v3, /device:TPU:1, one launch (start us, length us, event | category | flops | bytes accessed | tf_op | source)
XLA Modules:
  0.0 81.3 jit_solution(13607881255840937381)
XLA Ops:
  0.6 0.0 copy-start
  0.6 0.7 copy-done
  1.3 0.0 copy-start.1
  1.3 0.7 copy-done.1
  2.0 76.2 %shard_map.85 = (f32[2,256,256]{2,1,0:T(8,128)S(1)}, f32[8,256]{1,0:T(8,128)S(1)}, f32[1,1]{1,0:T(1,128)}) custom-call(s32[1,2]{1,0:T(1,128)S(1)} %copy-done.1, f32[8,256]{1,0:T(8,128)S(1)} %bitcast.8, f32[2,256,256]{2,1,0:T(8,128)} %bitcast.10, f32[4,256,256]{2,1,0:T(8,128)} %constant.6.clone.dft_in, f32[2,2,2,128,256]{4,3,2,1,0:T(8,128)} %constant.7.clone.wg_in, ...), custom_call_target="tpu_custom_call" | custom-call | tf_op jit(solution)/shard_map/pallas_call | solution.py:622
  78.2 0.8 copy.13
  79.0 0.6 copy.14
Async XLA Ops:
  0.6 0.7 copy-start
  1.3 0.7 copy-start.1

commit v4 on v3

--- a/solution.py
+++ b/solution.py
@@ -3,6 +3,7 @@
 
 import jax
 import jax.numpy as jnp
+import ml_dtypes
 import numpy as np
 from jax import lax
 from jax.experimental import pallas as pl
@@ -28,21 +29,46 @@
 
 
 ILLUM_STEPS = far_first(4, 8)
-CHIP_STEPS = [(dx, dy) for dy in (2, 0, 1, 3) for dx in (2, 1, 3, 0) if dx or dy]
+EARLY_STEPS = [(dx, dy) for dy in (2, 0) for dx in (2, 1, 3, 0) if dx or dy]
+LATE_STEPS = [(dx, dy) for dy in (1, 3) for dx in (2, 1, 3, 0)]
 ALL_STEPS = far_first(4, 8, 4)
 CHIPS = 128
 DEPTH_STEPS = sorted(range(1, 8), key=lambda k: -min(k, 8 - k))
 
 
+def balanced(c, s):
+    exact = c + 1j * s
+    near = [v.astype(ml_dtypes.bfloat16).astype(np.float64) for v in (c, s)]
+    step = [2.0 ** (np.floor(np.log2(np.maximum(np.abs(v), 1e-30))) - 7) for v in (c, s)]
+    away = [n + np.sign(v - n) * d for v, n, d in zip((c, s), near, step)]
+    away = [a.astype(ml_dtypes.bfloat16).astype(np.float64) for a in away]
+    out = near[0] + 1j * near[1]
+    change = np.concatenate([away[0] - near[0], 1j * (away[1] - near[1])]) * np.conj(np.concatenate([exact, exact]))
+    flipped = np.zeros(change.shape, bool)
+    for m in range(c.shape[1]):
+        bias = np.sum((out[:, m] - exact[:, m]) * np.conj(exact[:, m]))
+        for _ in range(24):
+            trial = np.abs(bias + np.where(flipped[:, m], np.inf, change[:, m].real) + 1j * change[:, m].imag)
+            best = np.argmin(trial)
+            if not trial[best] < np.abs(bias):
+                break
+            flipped[best, m] = True
+            bias = bias + change[best, m]
+    real, imag = flipped[: c.shape[0]], flipped[c.shape[0] :]
+    return np.where(real, away[0], near[0]), np.where(imag, away[1], near[1])
+
+
 def dft_tables():
     n = np.arange(H)[:, None]
     m = np.arange(H)[None, :]
-    out = []
+    out, light = [], []
     for q in (0, 1):
         theta = -2.0 * np.pi / N * ((n * (2 * m + q)) % N)
         c, s = np.cos(theta), np.sin(theta)
         out.append(np.block([[c, s], [-s, c]]))
-    return np.stack(out + [r.T for r in out]).astype(np.float32)
+        c, s = balanced(c, s)
+        light.append(np.block([[c, s], [-s, c]]))
+    return np.stack(out + [r.T for r in out] + light + [r.T for r in light]).astype(np.float32)
 
 
 def depth_tables():
@@ -73,9 +99,7 @@
 
 def dot_right(a, m_ref, q, exact=True):
     if not exact:
-        hi = a.astype(jnp.bfloat16)
-        m = jnp.concatenate([m_ref[q, 0], m_ref[q, 1]], axis=0)
-        return jnp.dot(jnp.concatenate([hi, hi], axis=1), m, preferred_element_type=jnp.float32)
+        return jnp.dot(a.astype(jnp.bfloat16), m_ref[q, 2], preferred_element_type=jnp.float32)
     hi, lo = split(a)
     mh, ml = m_ref[q, 0], m_ref[q, 1]
     return jnp.dot(
@@ -87,9 +111,7 @@
 
 def dot_left(m_ref, q, a, exact=True):
     if not exact:
-        hi = a.astype(jnp.bfloat16)
-        m = jnp.concatenate([m_ref[q, 0], m_ref[q, 1]], axis=1)
-        return jnp.dot(m, jnp.concatenate([hi, hi], axis=0), preferred_element_type=jnp.float32)
+        return jnp.dot(m_ref[q, 2], a.astype(jnp.bfloat16), preferred_element_type=jnp.float32)
     hi, lo = split(a)
     mh, ml = m_ref[q, 0], m_ref[q, 1]
     return jnp.dot(
@@ -197,33 +219,41 @@
     for k in range(1, NZ):
         greet(slab_peer(k))
 
-    z_rows = pl.ds(pl.multiple_of(z * 8, 8), 8)
     loads = [
         pltpu.make_async_copy(src, dst, in_sem.at[i])
         for i, (src, dst) in enumerate((
-            (block, zbuf.at[z_rows]), (angles_in, angles), (meas_in, meas), (dft_in, dft),
+            (angles_in, angles), (dft_in, dft), (meas_in, meas),
             (wg_in, wg), (source_table.at[slab], h7),
         ))
     ]
     for load in loads:
         load.start()
-    for load in loads[:4]:
-        load.wait()
-    for q in (0, 1):
-        for i, value in enumerate(split(dft[q])):
-            right[q, i] = value
-        for i, value in enumerate(split(dft[2 + q])):
-            left[q, i] = value
-
-    def store_mh(q, value):
-        mh[q, 0] = value[:H]
-        mh[q, 1] = value[H:]
-
-    forward_plane(meas[0], meas[1], right, left, store_mh)
     pl.semaphore_wait(barrier, 7 + 12 + 7)
 
+    high = slab // 4
+    slot = slab + high * (7 - 2 * slab)
+
+    def z_rows(k, n):
+        return pl.ds(pl.multiple_of(k * n, n), n)
+
+    def chip_peer(dx, dy):
+        return (illum_at(dx, 0), 2 * lax.rem(chip + dy, 4) + high)
+
     for dz in DEPTH_STEPS:
-        sent(zbuf.at[z_rows], zbuf.at[z_rows], ga_s, ga_r, (illum_at(0, dz), slab)).start()
+        sent(block, zbuf.at[z_rows(z, 8)], ga_s, ga_r.at[z], (illum_at(0, dz), slab)).start()
+    own_rows = pltpu.make_async_copy(block, zbuf.at[z_rows(z, 8)], ga_r.at[z])
+    own_rows.start()
+
+    def pass_on(step):
+        k = lax.rem(z // 2 + 4 + step, 4)
+        for i in (0, 1):
+            pltpu.make_async_copy(block, zbuf.at[z_rows(2 * k + i, 8)], ga_r.at[2 * k + i]).wait()
+        for dx, dy in EARLY_STEPS:
+            rows = pl.ds(pl.multiple_of(x * 64 + k * 16, 16), 16)
+            sent(zbuf.at[z_rows(k, 16)], c4.at[slot, rows], gb_s, gb_r.at[slot], chip_peer(dx, dy)).start()
+
+    near = 2 * lax.rem(z, 2) - 1
+    loads[0].wait()
 
     def angle_row(i):
         return jnp.sin(TILT * jnp.full((1, H), angles[0, i], jnp.int32).astype(jnp.float32))
@@ -260,17 +290,32 @@
 
     pl.loop(0, 4)(keep_incident)
 
-    wait_bytes(zbuf.at[pl.ds(0, 56)], ga_r)
-
-    high = slab // 4
-    slot = slab + high * (7 - 2 * slab)
-    x_rows = pl.ds(pl.multiple_of(x * 64, 64), 64)
-    for dx, dy in CHIP_STEPS:
-        dest = 2 * lax.rem(chip + dy, 4) + high
-        sent(zbuf, c4.at[slot, x_rows], gb_s, gb_r.at[slot], (illum_at(dx, 0), dest)).start()
+    pass_on(0)
+    pass_on(near)
+
+    def store_mh(q, value):
+        mh[q, 0] = value[:H]
+        mh[q, 1] = value[H:]
+
+    for load in loads[1:3]:
+        load.wait()
+    for q in (0, 1):
+        for i, value in enumerate(split(dft[q])):
+            right[q, i] = value
+        for i, value in enumerate(split(dft[2 + q])):
+            left[q, i] = value
+        right[q, 2] = dft[4 + q].astype(jnp.bfloat16)
+        left[q, 2] = dft[6 + q].astype(jnp.bfloat16)
+    pass_on(-near)
+    forward_plane(meas[0], meas[1], right, left, store_mh)
+    pass_on(2)
+
+    all_rows = pl.ds(pl.multiple_of(x * 64, 64), 64)
+    for dx, dy in LATE_STEPS:
+        sent(zbuf, c4.at[slot, all_rows], gb_s, gb_r.at[slot], chip_peer(dx, dy)).start()
 
     def to_other():
-        return sent(zbuf, c4.at[slot, x_rows], go_s, gb_r.at[slot], other)
+        return sent(zbuf, c4.at[slot, all_rows], go_s, gb_r.at[slot], other)
 
     @pl.when(core != high)
     def _():
@@ -278,7 +323,7 @@
 
     @pl.when(core == high)
     def _():
-        c4[slot, x_rows] = zbuf[...]
+        c4[slot, all_rows] = zbuf[...]
 
     def wait_plane(k):
         here = (core == high) & (slot == k)
@@ -304,8 +349,14 @@
         re, im = pair(wg, t, xp, rows=rows)
         return re, im if sign > 0 else -im
 
-    def exchange(n, xp):
-        return sent(f_buf.at[2, xp], ybuf.at[n, xp], x_s.at[n, xp], x_r.at[n, xp], other)
+    def chunks(n):
+        size = H // 2 if n == 0 else H
+        return [(xp, base, size) for xp in (0, 1) for base in range(0, H, size)]
+
+    def exchange(n, q):
+        xp, base, size = chunks(n)[q]
+        rows = pl.ds(base, size)
+        return sent(f_buf.at[2, xp, :, rows], ybuf.at[n, xp, :, rows], x_s.at[n, q], x_r.at[n, q], other)
 
     def forward_chained(p, re, im, n, exact=True):
         def store(q, value):
@@ -325,27 +376,27 @@
         wait_plane(p)
         c = c4[p]
         forward_plane(c * inc[p, 0], c * inc[p, 1], right, left, store_to(s_buf, p))
-    loads[4].wait()
-    for xp in (0, 1):
-
-        @pl.loop(0, H // 8)
+    loads[3].wait()
+    for q, (xp, base, size) in enumerate(chunks(0)):
+
+        @pl.loop(0, size // 16)
         def _(i):
-            rows = pl.ds(pl.multiple_of(i * 8, 8), 8)
+            rows = pl.ds(pl.multiple_of(base + i * 16, 16), 16)
             w = table(0, xp, 1, rows)
             f = pair(s_buf, 0, xp, rows=rows)
             for k in range(1, 4):
                 f = cadd(pair(s_buf, k, xp, rows=rows), cmul(w, f))
                 put(f_buf, f, k - 1, xp, rows=rows)
 
-        exchange(0, xp).start()
+        exchange(0, q).start()
     fields[0], fields[1] = incident(slab)
 
     def second_pass(src, n, sign, emit, acc):
-        for xp in (0, 1):
-            exchange(n, xp).wait()
+        for q, (xp, base, size) in enumerate(chunks(n)):
+            exchange(n, q).wait()
 
             def step(i, acc):
-                rows = pl.ds(pl.multiple_of(i * 8, 8), 8)
+                rows = pl.ds(pl.multiple_of(base + i * 16, 16), 16)
                 w, g = table(0, xp, sign, rows), table(1, xp, sign, rows)
                 t = pair(ybuf, n, xp, rows=rows)
                 out = [None] * 4
@@ -358,8 +409,8 @@
                         t = cadd(v, u)
                 return emit(out, xp, rows, acc)
 
-            acc = lax.fori_loop(0, H // 8, step, acc)
-            if emit.following is not None:
+            acc = lax.fori_loop(0, size // 16, step, acc)
+            if emit.following is not None and base + size == H:
                 exchange(emit.following, xp).start()
         return acc
 
@@ -378,7 +429,7 @@
 
             keep(p, *inverse_plane(load, right, left))
 
-    zero = jnp.zeros((8, N), jnp.float32)
+    zero = jnp.zeros((16, N), jnp.float32)
 
     def norm(acc, value):
         return acc + (value[0] * value[0] + value[1] * value[1])
@@ -538,7 +589,7 @@
         hat_copy().wait_recv()
         last_copy().wait_recv()
 
-    loads[5].wait()
+    loads[4].wait()
     last = 5 * (1 - core)
     forward_plane(g1[last, 0], g1[last, 1], right, left, store_to(gh1, 4))
     red2.wait()
@@ -631,9 +682,9 @@
         scratch_shapes=[
             pltpu.SMEM((1, 2), jnp.int32),
             pltpu.VMEM((2, N, N), f32),
-            pltpu.VMEM((4, N, N), f32),
-            pltpu.VMEM((2, 2, N, N), jnp.bfloat16),
-            pltpu.VMEM((2, 2, N, N), jnp.bfloat16),
+            pltpu.VMEM((8, N, N), f32),
+            pltpu.VMEM((2, 3, N, N), jnp.bfloat16),
+            pltpu.VMEM((2, 3, N, N), jnp.bfloat16),
             pltpu.VMEM((2, *spectral), f32),
             pltpu.VMEM((4, 2, N, N), f32),
             pltpu.VMEM((64, N), f32),
@@ -655,8 +706,8 @@
             pltpu.VMEM((ILLUMS, 8, N), f32),
             pltpu.VMEM((3, 1, H), f32),
             pltpu.VMEM((CHIPS, 1, H), f32),
-            dma((6,)), dma, dma, dma, dma, dma((4,)),
-            dma((5, 2)), dma((5, 2)),
+            dma((5,)), dma, dma((8,)), dma, dma, dma((4,)),
+            dma((5, 4)), dma((5, 4)),
             dma((3,)), dma((3,)), dma((2,)), dma((2,)), dma((2,)), dma((2,)),
             dma, dma, dma, dma, dma, dma,
         ],

time: 81.5 us -> 77.9 us (0.956)
  Pallas kernels: 76.2 us -> 72.6 us
    pallas_call x1, Pallas kernels: 76.2 us -> 72.6 us  [body(): pl.pallas_call(kernel, out_shape=(jax.ShapeDtypeStruct((2, N, N), f32), j...]
where the time goes in v4:
time: 77.9 us; the launch traced here: 77.7 us
  Pallas kernels  72.6 us (93%)
  local copies, waits for them, and re-layouts  2.74 us (4%)
  between operations  2.41 us (3%)
    pallas_call x1, Pallas kernels, body(): pl.pallas_call(kernel, out_shape=(jax.ShapeDtypeStruct((2, N, N), f32), j...  72.6 us
    unnamed x6, local copies, waits for them, and re-layouts  2.74 us

profile of v4, /device:TPU:1, one launch (start us, length us, event | category | flops | bytes accessed | tf_op | source)
XLA Modules:
  0.0 77.7 jit_solution(8953549350960240275)
XLA Ops:
  0.6 0.0 copy-start
  0.6 0.7 copy-done
  1.3 0.0 copy-start.1
  1.3 0.7 copy-done.1
  2.0 72.6 %shard_map.85 = (f32[2,256,256]{2,1,0:T(8,128)S(1)}, f32[8,256]{1,0:T(8,128)S(1)}, f32[1,1]{1,0:T(1,128)}) custom-call(s32[1,2]{1,0:T(1,128)S(1)} %copy-done.1, f32[8,256]{1,0:T(8,128)S(1)} %bitcast.8, f32[2,256,256]{2,1,0:T(8,128)} %bitcast.10, f32[8,256,256]{2,1,0:T(8,128)} %constant.6.clone.dft_in, f32[2,2,2,128,256]{4,3,2,1,0:T(8,128)} %constant.7.clone.wg_in, ...), custom_call_target="tpu_custom_call" | custom-call | tf_op jit(solution)/shard_map/pallas_call | solution.py:673
  74.6 0.8 %copy.13 = f32[1,2,1,256,256]{4,3,2,1,0:T(8,128)} copy(f32[1,2,1,256,256]{4,3,2,1,0:T(8,128)S(1)} %bitcast.7) | data formatting | bytes 1048576
  75.4 0.6 copy.14
Async XLA Ops:
  0.6 0.7 copy-start
  1.3 0.7 copy-start.1

commit v5 on v4

--- a/solution.py
+++ b/solution.py
@@ -31,8 +31,8 @@
 ILLUM_STEPS = far_first(4, 8)
 EARLY_STEPS = [(dx, dy) for dy in (2, 0) for dx in (2, 1, 3, 0) if dx or dy]
 LATE_STEPS = [(dx, dy) for dy in (1, 3) for dx in (2, 1, 3, 0)]
-ALL_STEPS = far_first(4, 8, 4)
-CHIPS = 128
+ALL_STEPS = far_first(4, 8, 4, 2)
+DEVICES = 256
 DEPTH_STEPS = sorted(range(1, 8), key=lambda k: -min(k, 8 - k))
 
 
@@ -182,7 +182,7 @@
     angles, meas, dft, right, left, wg, inc, zbuf, c4, s_buf, f_buf, w_buf, gh0, gh1, g0, g1, r_buf, ybuf, red_out, red_in,
     mh, h7, part, rs_in, ar_out, ar_in,
     in_sem, ga_s, ga_r, gb_s, go_s, gb_r, x_s, x_r, rd_s, rd_r, pg_s, pg_r, ht_s, ht_r,
-    rs_s, rs_r, a1_s, a1_r, a2_s, a2_r,
+    rs_s, rs_r, a2_s, a2_r,
 ):
     illum = lax.axis_index("illum")
     slab = lax.axis_index("slab")
@@ -632,18 +632,14 @@
         square_row + pltpu.roll(square_row, H // 2, 1),
         misfit_row + pltpu.roll(misfit_row, H // 2, 1),
     )
-    ar_out[0] = both
-    pair_sum = sent(ar_out.at[0], ar_out.at[1], a1_s, a1_r, other)
-    pair_sum.start()
-    pair_sum.wait_recv()
-    ar_out[2] = both + ar_out[1]
-    me = illum * 4 + chip
-    for dx, dz, dy in ALL_STEPS:
-        peer = (illum_at(dx, dz), 2 * lax.rem(chip + dy, 4) + core)
-        sent(ar_out.at[2], ar_in.at[me], a2_s, a2_r, peer).start()
-    ar_in[me] = ar_out[2]
-    wait_bytes(ar_in.at[pl.ds(0, CHIPS - 1)], a2_r)
-    sums = jnp.sum(ar_in[...], axis=0)
+    ar_out[...] = both
+    me = illum * NZ + slab
+    for dx, dz, dy, dc in ALL_STEPS:
+        peer = (illum_at(dx, dz), 2 * lax.rem(chip + dy, 4) + lax.rem(core + dc, 2))
+        sent(ar_out, ar_in.at[pl.ds(me, 1)], a2_s, a2_r, peer).start()
+    ar_in[pl.ds(me, 1)] = both
+    wait_bytes(ar_in.at[pl.ds(0, DEVICES - 1)], a2_r)
+    sums = jnp.sum(ar_in[...], axis=0, keepdims=True)
     square = jnp.sum(jnp.where(lane < H // 2, sums, 0.0), axis=1, keepdims=True)
     descent[...] = rows / jnp.sqrt(square * (1.0 / (NZ * N * N)) + 1e-06)
     misfit[0, 0] = jnp.sum(jnp.where(lane < H // 2, 0.0, sums))
@@ -657,8 +653,7 @@
     for _ in range(15):
         wait_bytes(zbuf, gb_s)
     wait_bytes(rs_in.at[pl.ds(0, ILLUMS - 1)], rs_s)
-    pair_sum.wait_send()
-    wait_bytes(ar_in.at[pl.ds(0, CHIPS - 1)], a2_s)
+    wait_bytes(ar_in.at[pl.ds(0, DEVICES - 1)], a2_s)
 
 
 def body(angles, contrast, measured):
@@ -704,12 +699,12 @@
             pltpu.VMEM(spectral, f32),
             pltpu.VMEM((N, N), f32),
             pltpu.VMEM((ILLUMS, 8, N), f32),
-            pltpu.VMEM((3, 1, H), f32),
-            pltpu.VMEM((CHIPS, 1, H), f32),
+            pltpu.VMEM((1, H), f32),
+            pltpu.VMEM((DEVICES, H), f32),
             dma((5,)), dma, dma((8,)), dma, dma, dma((4,)),
             dma((5, 4)), dma((5, 4)),
             dma((3,)), dma((3,)), dma((2,)), dma((2,)), dma((2,)), dma((2,)),
-            dma, dma, dma, dma, dma, dma,
+            dma, dma, dma, dma,
         ],
         compiler_params=pltpu.CompilerParams(
             collective_id=0, has_side_effects=True, vmem_limit_bytes=53 * 1024 * 1024,

time: 77.9 us -> 77.6 us (level)
  no operation moved by 1% of the time
where the time goes in v5:
time: 77.6 us; the launch traced here: 77.4 us
  Pallas kernels  72.3 us (93%)
  local copies, waits for them, and re-layouts  2.74 us (4%)
  between operations  2.41 us (3%)
    pallas_call x1, Pallas kernels, body(): pl.pallas_call(kernel, out_shape=(jax.ShapeDtypeStruct((2, N, N), f32), j...  72.3 us
    unnamed x6, local copies, waits for them, and re-layouts  2.74 us

profile of v5, /device:TPU:1, one launch (start us, length us, event | category | flops | bytes accessed | tf_op | source)
XLA Modules:
  0.0 77.4 jit_solution(16775930082471184892)
XLA Ops:
  0.6 0.0 copy-start
  0.6 0.7 copy-done
  1.3 0.0 copy-start.1
  1.3 0.7 copy-done.1
  2.0 72.3 %shard_map.85 = (f32[2,256,256]{2,1,0:T(8,128)S(1)}, f32[8,256]{1,0:T(8,128)S(1)}, f32[1,1]{1,0:T(1,128)}) custom-call(s32[1,2]{1,0:T(1,128)S(1)} %copy-done.1, f32[8,256]{1,0:T(8,128)S(1)} %bitcast.8, f32[2,256,256]{2,1,0:T(8,128)} %bitcast.10, f32[8,256,256]{2,1,0:T(8,128)} %constant.6.clone.dft_in, f32[2,2,2,128,256]{4,3,2,1,0:T(8,128)} %constant.7.clone.wg_in, ...), custom_call_target="tpu_custom_call" | custom-call | tf_op jit(solution)/shard_map/pallas_call | solution.py:668
  74.3 0.8 %copy.13 = f32[1,2,1,256,256]{4,3,2,1,0:T(8,128)} copy(f32[1,2,1,256,256]{4,3,2,1,0:T(8,128)S(1)} %bitcast.7) | data formatting | bytes 1048576
  75.1 0.6 copy.14
Async XLA Ops:
  0.6 0.7 copy-start
  1.3 0.7 copy-start.1
